TPU v7x, 256 devices: a whole 4x4x8 slice. The times are simulated.
256 devices in a mesh: row: 8 (over z_lo, core), col: 32 (over y, z_hi, x).
Axes of the slice: x: 4, y: 4, z: 8 (z_hi: 2, z_lo: 4; z = z_hi * 4 + z_lo), core: 2. Of those that a mesh axis runs over, the one named last changes fastest.
Arguments:
- a_blocks: float32 [8, 32, 48, 128, 128], P('row', 'col'), may hold values from -0.25 to 0.25
- b_blocks: float32 [8, 32, 48, 128, 128], P('row', 'col'), may hold values from -0.25 to 0.25
- c_prior: float32 [8, 32, 48, 128, 128], P('row', 'col'), may hold values from -6 to 6
- pair_a: int32 [8, 32, 2, 320], P('row', 'col'), may hold values from 0 to 47
- pair_b: int32 [8, 32, 2, 320], P('row', 'col'), may hold values from 0 to 47
- pair_c: int32 [8, 32, 2, 320], P('row', 'col'), may hold values from 0 to 47
- pair_count: int32 [8, 32, 2], P('row', 'col'), may hold values from 80 to 320
- diag_slot: int32 [8, 32], P('row', 'col'), may hold values from 0 to 47
Outputs:
- c_blocks: float32 [8, 32, 48, 128, 128], P('row', 'col')
- trace_value: float32 [], replicated
All inputs are finite; a program needn't handle non-finite values.
Results may differ from a plain program's by a relative error of at most 0.0003.
Values sent between devices are 32-bit elements; how exact they have to be, the bound alone decides.
No kernel may reach another device: no remote copies, remote signals or barrier semaphores. Data moves between devices by JAX's collectives and lax.ppermute only.
A program may use at most 128 MiB of HBM per device.

v0:
```python
import jax
import jax.numpy as jnp
from jax import lax
from jax.sharding import PartitionSpec as P


def passed_along(block, axis, distance):
    devices = range(lax.axis_size(axis))
    route = [((i - distance) % len(devices), i) for i in devices]
    return lax.ppermute(block, axis, route)


def pair_products(stores, acc, idx_a, idx_b, idx_c, counts):
    total_pairs = idx_a.shape[0]
    size = min(64, total_pairs)
    groups = total_pairs // size
    xs = (
        idx_a.reshape(groups, size),
        idx_b.reshape(groups, size),
        idx_c.reshape(groups, size),
        counts.reshape(groups, size),
    )

    def one_group(total, item):
        ga, gb, gc, gl = item
        left_pick = stores[0][0][ga]
        right_pick = stores[0][1][gb]
        prod = jnp.einsum("pij,pjk->pik", left_pick, right_pick, precision=lax.Precision.HIGHEST)
        return (total.at[gc].add(prod * gl[:, None, None]), None)

    result, _ = lax.scan(one_group, acc, xs)
    return result


def local(a_blocks, b_blocks, c_prior, pair_a, pair_b, pair_c, pair_count, diag_slot):
    left_here = a_blocks[0, 0]
    right_here = b_blocks[0, 0]
    c_now = c_prior[0, 0]
    total_pairs = pair_a.shape[3]
    position = jnp.arange(total_pairs, dtype=jnp.int32)
    left_next = passed_along(left_here, "col", -1)
    right_next = passed_along(right_here, "row", -1)
    live_first = (position < pair_count[0, 0, 0]).astype(jnp.float32)
    live_second = (position < pair_count[0, 0, 1]).astype(jnp.float32)
    c_now = pair_products(
        ((left_here, right_here),),
        c_now,
        pair_a[0, 0, 0],
        pair_b[0, 0, 0],
        pair_c[0, 0, 0],
        live_first,
    )
    c_now = pair_products(
        ((left_next, right_next),),
        c_now,
        pair_a[0, 0, 1],
        pair_b[0, 0, 1],
        pair_c[0, 0, 1],
        live_second,
    )
    chosen = lax.dynamic_index_in_dim(c_now, diag_slot[0, 0], 0, keepdims=False)
    local_trace = jnp.trace(chosen)
    total = lax.psum(local_trace, ("row", "col"))
    devices = lax.axis_size("row") * lax.axis_size("col")
    trace_value = total / (chosen.shape[0] * jnp.sqrt(jnp.float32(devices)))
    return (c_now[None, None], trace_value)


def solution(mesh):
    placed = (
        P("row", "col", None, None, None),
        P("row", "col", None, None, None),
        P("row", "col", None, None, None),
        P("row", "col", None, None),
        P("row", "col", None, None),
        P("row", "col", None, None),
        P("row", "col", None),
        P("row", "col"),
    )
    return jax.shard_map(
        local,
        mesh=mesh,
        in_specs=placed,
        out_specs=(P("row", "col", None, None, None), P()),
        check_vma=False,
    )
```

profile of v0, /device:TPU:1, one launch (start us, length us, event | category | flops | bytes accessed | tf_op | source)
XLA Modules:
  0.0 400.5 jit_solution(13742024978660616443)
XLA Ops:
  0.7 12.5 %collective-permute-start = (f32[48,128,128]{2,1,0:T(8,128)}, f32[48,128,128]{2,1,0:T(8,128)}, u32[]{:S(2)}, u32[]{:S(2)}) collective-permute-start(f32[48,128,128]{2,1,0:T(8,128)} %bitcast.15), channel_id=1, source_target_pairs={{1,0},{2,1},{3,2},{4,3},{5,4},{6,5},{7,6},{8,7},{9,8},{10,9},{11,1... | collective-permute-start | bytes 9437192 | tf_op jit(solution)/shard_map/ppermute | solution.py:10
  13.1 1.0 collective-permute-start.1
  15.9 0.7 fusion.18
  17.2 140.1 %while.20 = (s32[]{:T(128)}, f32[48,128,128]{2,1,0:T(8,128)S(1)}, s32[5,64]{1,0:T(8,128)S(1)}, s32[5,64]{1,0:T(8,128)S(1)}, f32[48,128,128]{2,1,0:T(8,128)}, /*i...) while((s32[]{:T(128)}, f32[48,128,128]{2,1,0:T(8,128)S(1)}, ...), condition=%wide.region_2.3_spmd, body=%wide.region_0.2_spmd.sunk | while | flops 1612712576 | bytes 41954928 | solution.py:31
  17.3 4.6 %gather_fusion = f32[64,128,128]{2,1,0:T(8,128)} fusion(f32[48,128,128]{2,1,0:T(8,128)} %get-tuple-element.260, s32[1024]{0:T(1024)S(1)} %pad_clamp_fusion.8), kind=kCustom, calls=%fused_computation.clone.1 | custom fusion | bytes 8388864 | tf_op jit(solution)/shard_map/while/body/eval_jaxpr/gather | solution.py:26
  21.9 4.7 %gather_fusion.1 = f32[64,128,128]{2,1,0:T(8,128)} fusion(f32[48,128,128]{2,1,0:T(8,128)} %get-tuple-element.262, s32[1024]{0:T(1024)S(1)} %pad_clamp_fusion.9), kind=kCustom, calls=%fused_computation.1.clone.1 | custom fusion | bytes 8388864 | tf_op jit(solution)/shard_map/while/body/eval_jaxpr/gather | solution.py:27
  26.6 9.8 %convolution_multiply_fusion.4 = f32[64,128,128]{2,1,0:T(8,128)} fusion(f32[64,128,128]{2,1,0:T(8,128)} %gather_fusion, f32[64,128,128]{2,1,0:T(8,128)} %gather_fusion.1, f32[64]{0:T(128)S(1)} %fusion.38), kind=kOutput, calls=%fused_computation.6.clone.1 | convolution fusion | flops 1611661312 | bytes 12583168 | tf_op jit(solution)/shard_map/while/body/eval_jaxpr/pij,pjk->pik/dot_general | solution.py:28
  36.4 8.8 %scatter_fusion = f32[48,128,128]{2,1,0:T(8,128)S(1)} fusion(f32[48,128,128]{2,1,0:T(8,128)S(1)} %get-tuple-element.248, s32[64]{0:T(128)S(1)} %get-tuple-element.226, f32[64,128,128]{2,1,0:T(8,128)} %convolution_multiply_fusion.4), kind=kCustom, calls=%fused_computation.4.clone.1 | custom fusion | flops 1048576 | bytes 12583168 | tf_op jit(solution)/shard_map/while/body/eval_jaxpr/scatter-add | solution.py:29
  45.3 4.6 %gather_fusion = f32[64,128,128]{2,1,0:T(8,128)} fusion(f32[48,128,128]{2,1,0:T(8,128)} %get-tuple-element.260, s32[1024]{0:T(1024)S(1)} %pad_clamp_fusion.8), kind=kCustom, calls=%fused_computation.clone.1 | custom fusion | bytes 8388864 | tf_op jit(solution)/shard_map/while/body/eval_jaxpr/gather | solution.py:26
  49.9 4.7 %gather_fusion.1 = f32[64,128,128]{2,1,0:T(8,128)} fusion(f32[48,128,128]{2,1,0:T(8,128)} %get-tuple-element.262, s32[1024]{0:T(1024)S(1)} %pad_clamp_fusion.9), kind=kCustom, calls=%fused_computation.1.clone.1 | custom fusion | bytes 8388864 | tf_op jit(solution)/shard_map/while/body/eval_jaxpr/gather | solution.py:27
  54.6 9.8 %convolution_multiply_fusion.4 = f32[64,128,128]{2,1,0:T(8,128)} fusion(f32[64,128,128]{2,1,0:T(8,128)} %gather_fusion, f32[64,128,128]{2,1,0:T(8,128)} %gather_fusion.1, f32[64]{0:T(128)S(1)} %fusion.38), kind=kOutput, calls=%fused_computation.6.clone.1 | convolution fusion | flops 1611661312 | bytes 12583168 | tf_op jit(solution)/shard_map/while/body/eval_jaxpr/pij,pjk->pik/dot_general | solution.py:28
  64.5 8.8 %scatter_fusion = f32[48,128,128]{2,1,0:T(8,128)S(1)} fusion(f32[48,128,128]{2,1,0:T(8,128)S(1)} %get-tuple-element.248, s32[64]{0:T(128)S(1)} %get-tuple-element.226, f32[64,128,128]{2,1,0:T(8,128)} %convolution_multiply_fusion.4), kind=kCustom, calls=%fused_computation.4.clone.1 | custom fusion | flops 1048576 | bytes 12583168 | tf_op jit(solution)/shard_map/while/body/eval_jaxpr/scatter-add | solution.py:29
  73.3 4.6 %gather_fusion = f32[64,128,128]{2,1,0:T(8,128)} fusion(f32[48,128,128]{2,1,0:T(8,128)} %get-tuple-element.260, s32[1024]{0:T(1024)S(1)} %pad_clamp_fusion.8), kind=kCustom, calls=%fused_computation.clone.1 | custom fusion | bytes 8388864 | tf_op jit(solution)/shard_map/while/body/eval_jaxpr/gather | solution.py:26
  78.0 4.7 %gather_fusion.1 = f32[64,128,128]{2,1,0:T(8,128)} fusion(f32[48,128,128]{2,1,0:T(8,128)} %get-tuple-element.262, s32[1024]{0:T(1024)S(1)} %pad_clamp_fusion.9), kind=kCustom, calls=%fused_computation.1.clone.1 | custom fusion | bytes 8388864 | tf_op jit(solution)/shard_map/while/body/eval_jaxpr/gather | solution.py:27
  82.6 9.8 %convolution_multiply_fusion.4 = f32[64,128,128]{2,1,0:T(8,128)} fusion(f32[64,128,128]{2,1,0:T(8,128)} %gather_fusion, f32[64,128,128]{2,1,0:T(8,128)} %gather_fusion.1, f32[64]{0:T(128)S(1)} %fusion.38), kind=kOutput, calls=%fused_computation.6.clone.1 | convolution fusion | flops 1611661312 | bytes 12583168 | tf_op jit(solution)/shard_map/while/body/eval_jaxpr/pij,pjk->pik/dot_general | solution.py:28
  92.5 8.8 %scatter_fusion = f32[48,128,128]{2,1,0:T(8,128)S(1)} fusion(f32[48,128,128]{2,1,0:T(8,128)S(1)} %get-tuple-element.248, s32[64]{0:T(128)S(1)} %get-tuple-element.226, f32[64,128,128]{2,1,0:T(8,128)} %convolution_multiply_fusion.4), kind=kCustom, calls=%fused_computation.4.clone.1 | custom fusion | flops 1048576 | bytes 12583168 | tf_op jit(solution)/shard_map/while/body/eval_jaxpr/scatter-add | solution.py:29
  101.3 4.6 %gather_fusion = f32[64,128,128]{2,1,0:T(8,128)} fusion(f32[48,128,128]{2,1,0:T(8,128)} %get-tuple-element.260, s32[1024]{0:T(1024)S(1)} %pad_clamp_fusion.8), kind=kCustom, calls=%fused_computation.clone.1 | custom fusion | bytes 8388864 | tf_op jit(solution)/shard_map/while/body/eval_jaxpr/gather | solution.py:26
  106.0 4.7 %gather_fusion.1 = f32[64,128,128]{2,1,0:T(8,128)} fusion(f32[48,128,128]{2,1,0:T(8,128)} %get-tuple-element.262, s32[1024]{0:T(1024)S(1)} %pad_clamp_fusion.9), kind=kCustom, calls=%fused_computation.1.clone.1 | custom fusion | bytes 8388864 | tf_op jit(solution)/shard_map/while/body/eval_jaxpr/gather | solution.py:27
  110.7 9.8 %convolution_multiply_fusion.4 = f32[64,128,128]{2,1,0:T(8,128)} fusion(f32[64,128,128]{2,1,0:T(8,128)} %gather_fusion, f32[64,128,128]{2,1,0:T(8,128)} %gather_fusion.1, f32[64]{0:T(128)S(1)} %fusion.38), kind=kOutput, calls=%fused_computation.6.clone.1 | convolution fusion | flops 1611661312 | bytes 12583168 | tf_op jit(solution)/shard_map/while/body/eval_jaxpr/pij,pjk->pik/dot_general | solution.py:28
  120.5 8.8 %scatter_fusion = f32[48,128,128]{2,1,0:T(8,128)S(1)} fusion(f32[48,128,128]{2,1,0:T(8,128)S(1)} %get-tuple-element.248, s32[64]{0:T(128)S(1)} %get-tuple-element.226, f32[64,128,128]{2,1,0:T(8,128)} %convolution_multiply_fusion.4), kind=kCustom, calls=%fused_computation.4.clone.1 | custom fusion | flops 1048576 | bytes 12583168 | tf_op jit(solution)/shard_map/while/body/eval_jaxpr/scatter-add | solution.py:29
  129.4 4.6 %gather_fusion = f32[64,128,128]{2,1,0:T(8,128)} fusion(f32[48,128,128]{2,1,0:T(8,128)} %get-tuple-element.260, s32[1024]{0:T(1024)S(1)} %pad_clamp_fusion.8), kind=kCustom, calls=%fused_computation.clone.1 | custom fusion | bytes 8388864 | tf_op jit(solution)/shard_map/while/body/eval_jaxpr/gather | solution.py:26
  134.0 4.7 %gather_fusion.1 = f32[64,128,128]{2,1,0:T(8,128)} fusion(f32[48,128,128]{2,1,0:T(8,128)} %get-tuple-element.262, s32[1024]{0:T(1024)S(1)} %pad_clamp_fusion.9), kind=kCustom, calls=%fused_computation.1.clone.1 | custom fusion | bytes 8388864 | tf_op jit(solution)/shard_map/while/body/eval_jaxpr/gather | solution.py:27
  138.7 9.8 %convolution_multiply_fusion.4 = f32[64,128,128]{2,1,0:T(8,128)} fusion(f32[64,128,128]{2,1,0:T(8,128)} %gather_fusion, f32[64,128,128]{2,1,0:T(8,128)} %gather_fusion.1, f32[64]{0:T(128)S(1)} %fusion.38), kind=kOutput, calls=%fused_computation.6.clone.1 | convolution fusion | flops 1611661312 | bytes 12583168 | tf_op jit(solution)/shard_map/while/body/eval_jaxpr/pij,pjk->pik/dot_general | solution.py:28
  148.5 8.8 %scatter_fusion = f32[48,128,128]{2,1,0:T(8,128)S(1)} fusion(f32[48,128,128]{2,1,0:T(8,128)S(1)} %get-tuple-element.248, s32[64]{0:T(128)S(1)} %get-tuple-element.226, f32[64,128,128]{2,1,0:T(8,128)} %convolution_multiply_fusion.4), kind=kCustom, calls=%fused_computation.4.clone.1 | custom fusion | flops 1048576 | bytes 12583168 | tf_op jit(solution)/shard_map/while/body/eval_jaxpr/scatter-add | solution.py:29
  157.3 26.3 %collective-permute-done.1 = f32[48,128,128]{2,1,0:T(8,128)} collective-permute-done((f32[48,128,128]{2,1,0:T(8,128)}, f32[48,128,128]{2,1,0:T(8,128)}, u32[]{:S(2)}, u32[]{:S(2)}) %collective-permute-start.1) | collective-permute-done | bytes 3145760 | tf_op jit(solution)/shard_map/ppermute | solution.py:10
  183.7 140.1 %while.21 = (s32[]{:T(128)}, f32[48,128,128]{2,1,0:T(8,128)S(1)}, s32[5,64]{1,0:T(8,128)S(1)}, s32[5,64]{1,0:T(8,128)S(1)}, f32[48,128,128]{2,1,0:T(8,128)}, /*i...) while((s32[]{:T(128)}, f32[48,128,128]{2,1,0:T(8,128)S(1)}, ...), condition=%wide.region_5.6_spmd, body=%wide.region_3.5_spmd.sunk | while | flops 1612712576 | bytes 41954928 | solution.py:31
  183.7 4.6 %gather_fusion.2 = f32[64,128,128]{2,1,0:T(8,128)} fusion(f32[48,128,128]{2,1,0:T(8,128)} %get-tuple-element.287, s32[1024]{0:T(1024)S(1)} %pad_clamp_fusion.10), kind=kCustom, calls=%fused_computation.2.clone.1 | custom fusion | bytes 8388864 | tf_op jit(solution)/shard_map/while/body/eval_jaxpr/gather | solution.py:26
  188.3 4.7 %gather_fusion.3 = f32[64,128,128]{2,1,0:T(8,128)} fusion(f32[48,128,128]{2,1,0:T(8,128)} %get-tuple-element.289, s32[1024]{0:T(1024)S(1)} %pad_clamp_fusion.11), kind=kCustom, calls=%fused_computation.3.clone.1 | custom fusion | bytes 8388864 | tf_op jit(solution)/shard_map/while/body/eval_jaxpr/gather | solution.py:27
  193.0 9.8 %convolution_multiply_fusion.5 = f32[64,128,128]{2,1,0:T(8,128)} fusion(f32[64,128,128]{2,1,0:T(8,128)} %gather_fusion.2, f32[64,128,128]{2,1,0:T(8,128)} %gather_fusion.3, f32[64]{0:T(128)S(1)} %fusion.43), kind=kOutput, calls=%fused_computation.23.clone.1 | convolution fusion | flops 1611661312 | bytes 12583168 | tf_op jit(solution)/shard_map/while/body/eval_jaxpr/pij,pjk->pik/dot_general | solution.py:28
  202.9 8.8 %scatter_fusion.1 = f32[48,128,128]{2,1,0:T(8,128)S(1)} fusion(f32[48,128,128]{2,1,0:T(8,128)S(1)} %get-tuple-element.275, s32[64]{0:T(128)S(1)} %get-tuple-element.236, f32[64,128,128]{2,1,0:T(8,128)} %convolution_multiply_fusion.5), kind=kCustom, calls=%fused_computation.5.clone.1 | custom fusion | flops 1048576 | bytes 12583168 | tf_op jit(solution)/shard_map/while/body/eval_jaxpr/scatter-add | solution.py:29
  211.7 4.6 %gather_fusion.2 = f32[64,128,128]{2,1,0:T(8,128)} fusion(f32[48,128,128]{2,1,0:T(8,128)} %get-tuple-element.287, s32[1024]{0:T(1024)S(1)} %pad_clamp_fusion.10), kind=kCustom, calls=%fused_computation.2.clone.1 | custom fusion | bytes 8388864 | tf_op jit(solution)/shard_map/while/body/eval_jaxpr/gather | solution.py:26
  216.4 4.7 %gather_fusion.3 = f32[64,128,128]{2,1,0:T(8,128)} fusion(f32[48,128,128]{2,1,0:T(8,128)} %get-tuple-element.289, s32[1024]{0:T(1024)S(1)} %pad_clamp_fusion.11), kind=kCustom, calls=%fused_computation.3.clone.1 | custom fusion | bytes 8388864 | tf_op jit(solution)/shard_map/while/body/eval_jaxpr/gather | solution.py:27
  221.0 9.8 %convolution_multiply_fusion.5 = f32[64,128,128]{2,1,0:T(8,128)} fusion(f32[64,128,128]{2,1,0:T(8,128)} %gather_fusion.2, f32[64,128,128]{2,1,0:T(8,128)} %gather_fusion.3, f32[64]{0:T(128)S(1)} %fusion.43), kind=kOutput, calls=%fused_computation.23.clone.1 | convolution fusion | flops 1611661312 | bytes 12583168 | tf_op jit(solution)/shard_map/while/body/eval_jaxpr/pij,pjk->pik/dot_general | solution.py:28
  230.9 8.8 %scatter_fusion.1 = f32[48,128,128]{2,1,0:T(8,128)S(1)} fusion(f32[48,128,128]{2,1,0:T(8,128)S(1)} %get-tuple-element.275, s32[64]{0:T(128)S(1)} %get-tuple-element.236, f32[64,128,128]{2,1,0:T(8,128)} %convolution_multiply_fusion.5), kind=kCustom, calls=%fused_computation.5.clone.1 | custom fusion | flops 1048576 | bytes 12583168 | tf_op jit(solution)/shard_map/while/body/eval_jaxpr/scatter-add | solution.py:29
  239.7 4.6 %gather_fusion.2 = f32[64,128,128]{2,1,0:T(8,128)} fusion(f32[48,128,128]{2,1,0:T(8,128)} %get-tuple-element.287, s32[1024]{0:T(1024)S(1)} %pad_clamp_fusion.10), kind=kCustom, calls=%fused_computation.2.clone.1 | custom fusion | bytes 8388864 | tf_op jit(solution)/shard_map/while/body/eval_jaxpr/gather | solution.py:26
  244.4 4.7 %gather_fusion.3 = f32[64,128,128]{2,1,0:T(8,128)} fusion(f32[48,128,128]{2,1,0:T(8,128)} %get-tuple-element.289, s32[1024]{0:T(1024)S(1)} %pad_clamp_fusion.11), kind=kCustom, calls=%fused_computation.3.clone.1 | custom fusion | bytes 8388864 | tf_op jit(solution)/shard_map/while/body/eval_jaxpr/gather | solution.py:27
  249.1 9.8 %convolution_multiply_fusion.5 = f32[64,128,128]{2,1,0:T(8,128)} fusion(f32[64,128,128]{2,1,0:T(8,128)} %gather_fusion.2, f32[64,128,128]{2,1,0:T(8,128)} %gather_fusion.3, f32[64]{0:T(128)S(1)} %fusion.43), kind=kOutput, calls=%fused_computation.23.clone.1 | convolution fusion | flops 1611661312 | bytes 12583168 | tf_op jit(solution)/shard_map/while/body/eval_jaxpr/pij,pjk->pik/dot_general | solution.py:28
  258.9 8.8 %scatter_fusion.1 = f32[48,128,128]{2,1,0:T(8,128)S(1)} fusion(f32[48,128,128]{2,1,0:T(8,128)S(1)} %get-tuple-element.275, s32[64]{0:T(128)S(1)} %get-tuple-element.236, f32[64,128,128]{2,1,0:T(8,128)} %convolution_multiply_fusion.5), kind=kCustom, calls=%fused_computation.5.clone.1 | custom fusion | flops 1048576 | bytes 12583168 | tf_op jit(solution)/shard_map/while/body/eval_jaxpr/scatter-add | solution.py:29
  267.7 4.6 %gather_fusion.2 = f32[64,128,128]{2,1,0:T(8,128)} fusion(f32[48,128,128]{2,1,0:T(8,128)} %get-tuple-element.287, s32[1024]{0:T(1024)S(1)} %pad_clamp_fusion.10), kind=kCustom, calls=%fused_computation.2.clone.1 | custom fusion | bytes 8388864 | tf_op jit(solution)/shard_map/while/body/eval_jaxpr/gather | solution.py:26
  272.4 4.7 %gather_fusion.3 = f32[64,128,128]{2,1,0:T(8,128)} fusion(f32[48,128,128]{2,1,0:T(8,128)} %get-tuple-element.289, s32[1024]{0:T(1024)S(1)} %pad_clamp_fusion.11), kind=kCustom, calls=%fused_computation.3.clone.1 | custom fusion | bytes 8388864 | tf_op jit(solution)/shard_map/while/body/eval_jaxpr/gather | solution.py:27
  277.1 9.8 %convolution_multiply_fusion.5 = f32[64,128,128]{2,1,0:T(8,128)} fusion(f32[64,128,128]{2,1,0:T(8,128)} %gather_fusion.2, f32[64,128,128]{2,1,0:T(8,128)} %gather_fusion.3, f32[64]{0:T(128)S(1)} %fusion.43), kind=kOutput, calls=%fused_computation.23.clone.1 | convolution fusion | flops 1611661312 | bytes 12583168 | tf_op jit(solution)/shard_map/while/body/eval_jaxpr/pij,pjk->pik/dot_general | solution.py:28
  286.9 8.8 %scatter_fusion.1 = f32[48,128,128]{2,1,0:T(8,128)S(1)} fusion(f32[48,128,128]{2,1,0:T(8,128)S(1)} %get-tuple-element.275, s32[64]{0:T(128)S(1)} %get-tuple-element.236, f32[64,128,128]{2,1,0:T(8,128)} %convolution_multiply_fusion.5), kind=kCustom, calls=%fused_computation.5.clone.1 | custom fusion | flops 1048576 | bytes 12583168 | tf_op jit(solution)/shard_map/while/body/eval_jaxpr/scatter-add | solution.py:29
  295.8 4.6 %gather_fusion.2 = f32[64,128,128]{2,1,0:T(8,128)} fusion(f32[48,128,128]{2,1,0:T(8,128)} %get-tuple-element.287, s32[1024]{0:T(1024)S(1)} %pad_clamp_fusion.10), kind=kCustom, calls=%fused_computation.2.clone.1 | custom fusion | bytes 8388864 | tf_op jit(solution)/shard_map/while/body/eval_jaxpr/gather | solution.py:26
  300.4 4.7 %gather_fusion.3 = f32[64,128,128]{2,1,0:T(8,128)} fusion(f32[48,128,128]{2,1,0:T(8,128)} %get-tuple-element.289, s32[1024]{0:T(1024)S(1)} %pad_clamp_fusion.11), kind=kCustom, calls=%fused_computation.3.clone.1 | custom fusion | bytes 8388864 | tf_op jit(solution)/shard_map/while/body/eval_jaxpr/gather | solution.py:27
  305.1 9.8 %convolution_multiply_fusion.5 = f32[64,128,128]{2,1,0:T(8,128)} fusion(f32[64,128,128]{2,1,0:T(8,128)} %gather_fusion.2, f32[64,128,128]{2,1,0:T(8,128)} %gather_fusion.3, f32[64]{0:T(128)S(1)} %fusion.43), kind=kOutput, calls=%fused_computation.23.clone.1 | convolution fusion | flops 1611661312 | bytes 12583168 | tf_op jit(solution)/shard_map/while/body/eval_jaxpr/pij,pjk->pik/dot_general | solution.py:28
  314.9 8.8 %scatter_fusion.1 = f32[48,128,128]{2,1,0:T(8,128)S(1)} fusion(f32[48,128,128]{2,1,0:T(8,128)S(1)} %get-tuple-element.275, s32[64]{0:T(128)S(1)} %get-tuple-element.236, f32[64,128,128]{2,1,0:T(8,128)} %convolution_multiply_fusion.5), kind=kCustom, calls=%fused_computation.5.clone.1 | custom fusion | flops 1048576 | bytes 12583168 | tf_op jit(solution)/shard_map/while/body/eval_jaxpr/scatter-add | solution.py:29
  323.7 0.7 fusion.14
  324.5 74.2 %psum.7 = f32[]{:T(128)} all-reduce(f32[]{:T(128)} %fusion.14), channel_id=1, replica_groups=mesh['row'=8,'col'=32] {'row','col'}, use_global_device_ids=true, to_apply=%region_7.8 | all-reduce | flops 1 | bytes 8 | tf_op jit(solution)/shard_map/psum | solution.py:63
  (74 shorter events, 2.1 us)
Async XLA Ops:
  0.6 16.6 %copy-start.1 = (f32[1,1,48,128,128]{4,3,2,1,0:T(8,128)S(1)}, f32[1,1,48,128,128]{4,3,2,1,0:T(8,128)}, u32[]{:S(2)}) copy-start(f32[1,1,48,128,128]{4,3,2,1,0:T(8,128)} %param.14) | copy-start | bytes 9437188
  0.6 13.6 %copy-start.3 = (s32[1,1,2,320]{3,2,1,0:T(2,128)S(1)}, s32[1,1,2,320]{3,2,1,0:T(2,128)}, u32[]{:S(2)}) copy-start(s32[1,1,2,320]{3,2,1,0:T(2,128)} %param.15) | copy-start | bytes 7684
  0.7 13.7 %copy-start.4 = (s32[1,1,2,320]{3,2,1,0:T(2,128)S(1)}, s32[1,1,2,320]{3,2,1,0:T(2,128)}, u32[]{:S(2)}) copy-start(s32[1,1,2,320]{3,2,1,0:T(2,128)} %param.16) | copy-start | bytes 7684
  0.7 13.4 %copy-start.2 = (s32[1,1,2,320]{3,2,1,0:T(2,128)S(1)}, s32[1,1,2,320]{3,2,1,0:T(2,128)}, u32[]{:S(2)}) copy-start(s32[1,1,2,320]{3,2,1,0:T(2,128)} %param.17) | copy-start | bytes 7684
  0.7 13.7 %copy-start.5 = (s32[1,1,2]{2,1,0:T(1,128)S(1)}, s32[1,1,2]{2,1,0:T(1,128)}, u32[]{:S(2)}) copy-start(s32[1,1,2]{2,1,0:T(1,128)} %param.18) | copy-start | bytes 28
  0.7 156.7 %collective-permute-start = (f32[48,128,128]{2,1,0:T(8,128)}, f32[48,128,128]{2,1,0:T(8,128)}, u32[]{:S(2)}, u32[]{:S(2)}) collective-permute-start(f32[48,128,128]{2,1,0:T(8,128)} %bitcast.15), channel_id=1, source_target_pairs={{1,0},{2,1},{3,2},{4,3},{5,4},{6,5},{7,6},{8,7},{9,8},{10,9},{11,1... | collective-permute-start | bytes 9437192 | tf_op jit(solution)/shard_map/ppermute | solution.py:10
  13.1 170.5 %collective-permute-start.1 = (f32[48,128,128]{2,1,0:T(8,128)}, f32[48,128,128]{2,1,0:T(8,128)}, u32[]{:S(2)}, u32[]{:S(2)}) collective-permute-start(f32[48,128,128]{2,1,0:T(8,128)} %bitcast.16), channel_id=1, source_target_pairs={{32,0},{64,32},{96,64},{128,96},{160,128},{192,160},{224,192},{0,2... | collective-permute-start | bytes 9437192 | tf_op jit(solution)/shard_map/ppermute | solution.py:10
  323.7 75.6 %copy-start = (f32[48,128,128]{2,1,0:T(8,128)}, f32[48,128,128]{2,1,0:T(8,128)S(1)}, u32[]{:S(2)}) copy-start(f32[48,128,128]{2,1,0:T(8,128)S(1)} %get-tuple-element.87) | copy-start | bytes 9437188
where the time goes:
time: 403 us; the launch traced here: 400 us
  matrix products  98.4 us (24%)
  local copies, waits for them, and re-layouts  94.3 us (23%)
  other arithmetic  90.3 us (22%)
  blocking collectives  74.2 us (18%)
  waiting for transfers between devices  26.3 us (7%)
  starting transfers between devices  13.4 us (3%)
    dot_general x10, matrix products, one_group(): jnp.einsum('pij,pjk->pik', left_pick, right_pick, precision=lax.Precision...  98.4 us
    scatter-add x10, other arithmetic, one_group(): return (total.at[gc].add(prod * gl[:, None, None]), None)  88 us
    psum x1, blocking collectives, local(): total = lax.psum(local_trace, ('row', 'col'))  74.2 us
    gather x10, local copies, waits for them, and re-layouts, one_group(): right_pick = stores[0][1][gb]  46.7 us
    gather x10, local copies, waits for them, and re-layouts, one_group(): left_pick = stores[0][0][ga]  46.3 us
    ppermute x2, waiting for transfers between devices, passed_along(): return lax.ppermute(block, axis, route)  26.3 us
    ppermute x2, starting transfers between devices, passed_along(): return lax.ppermute(block, axis, route)  13.4 us
  transfers between devices with their start and end apart: 2, of which 1 were waited for; matrix products, arithmetic and copies ran while one was open for 36% of the time, Pallas kernels for 0%

commit v1 on v0

v1 whole, which is shorter than its diff:
```python
import jax
import jax.numpy as jnp
from jax import lax
from jax.experimental import pallas as pl
from jax.experimental.pallas import tpu as pltpu
from jax.sharding import PartitionSpec as P

AXES = ("row", "col")
BS = 128
UNROLL = 32
MIB = 2**20


def coords(device):
    row, col = divmod(device, 32)
    z_lo, core = divmod(row, 2)
    y, low = divmod(col, 8)
    z_hi, x = divmod(low, 4)
    return x, y, z_hi * 4 + z_lo, core


def device_at(x, y, z, core):
    x, y, z = x % 4, y % 4, z % 8
    return ((z % 4) * 2 + core) * 32 + (y * 2 + z // 4) * 4 + x


def route(chosen, move):
    pairs = []
    for device in range(256):
        place = coords(device)
        if chosen(*place):
            pairs.append((device, device_at(*move(*place))))
    return pairs


def y_of(y, z):
    return y if z >= 4 else y - 1


INNER = route(lambda x, y, z, k: x >= 1, lambda x, y, z, k: (x - 1, y, z, k))
RING = INNER + route(lambda x, y, z, k: x == 0, lambda x, y, z, k: (3, y_of(y, z), z, k))
TO_2 = route(lambda x, y, z, k: x == 0, lambda x, y, z, k: (2, y_of(y, z), z, k))
DIRECT = route(lambda x, y, z, k: x == 0, lambda x, y, z, k: (3, y_of(y, z), z + 4, k))
FROM_2 = route(lambda x, y, z, k: x == 2, lambda x, y, z, k: (3, y, z + 4, k))
FROM_3 = route(lambda x, y, z, k: x == 3, lambda x, y, z, k: (3, y, z + 4, k))
ROWS = [((i + 1) % 8, i) for i in range(8)]


def split(value):
    high = value.astype(jnp.bfloat16)
    return high, (value - high.astype(jnp.float32)).astype(jnp.bfloat16)


def multiply(step, idx_a, idx_b, idx_c, count, left, right, acc):
    live = count[0, 0, step]

    def product(pair):
        halves = left[idx_a[0, 0, step, pair]]
        weights = right[idx_b[0, 0, step, pair]]
        both = jnp.dot(halves, jnp.concatenate([weights, weights], axis=0), preferred_element_type=jnp.float32)
        return both[:, :BS] + both[:, BS:]

    def group(g, carry):
        for u in range(UNROLL):
            pair = g * UNROLL + u
            slot = jnp.where(pair < live, idx_c[0, 0, step, pair], acc.shape[0] - 1)
            acc[slot] = acc[slot] + product(pair)
        return carry

    lax.fori_loop(0, lax.div(live + UNROLL - 1, UNROLL), group, 0)


def load(source, target, sem):
    copy = pltpu.make_async_copy(source, target, sem)
    copy.start()
    return copy


def halve(source, target, start, size):
    def one(i, carry):
        high, low = split(source[i])
        target[i, :, 0:BS] = high
        target[i, :, BS:] = low
        return carry

    lax.fori_loop(start, start + size, one, 0, unroll=4)


def first_kernel(idx_a, idx_b, idx_c, count, a_ref, b_ref, c_ref, out_ref, a_in, b_in, left, right, acc, sems):
    blocks = a_in.shape[0]
    copies = [
        load(a_ref.at[0, 0], a_in, sems.at[0]),
        load(b_ref.at[0, 0], b_in, sems.at[1]),
        load(c_ref.at[0, 0], acc.at[pl.ds(0, blocks)], sems.at[2]),
    ]
    copies[0].wait()
    halve(a_in, left, 0, blocks)
    copies[1].wait()
    halve(b_in, right, 0, blocks)
    copies[2].wait()
    multiply(0, idx_a, idx_b, idx_c, count, left, right, acc)
    load(acc.at[pl.ds(0, blocks)], out_ref, sems.at[3]).wait()


def second_kernel(
    idx_a, idx_b, idx_c, count, diag, wraps,
    first_in, first_wrap, rest_in, mid_wrap, last_wrap, b_ref, c_ref,
    out_ref, trace_ref, a_in, b_in, left, right, acc, sems,
):
    blocks = a_in.shape[0]
    third = blocks // 3
    spots = [a_in.at[pl.ds(i * third, third)] for i in range(3)]
    b_copy = load(b_ref.at[0, 0], b_in, sems.at[3])
    c_copy = load(c_ref, acc.at[pl.ds(0, blocks)], sems.at[4])
    inner = [first_in, rest_in.at[pl.ds(0, third)], rest_in.at[pl.ds(third, third)]]
    wrapped = [first_wrap, mid_wrap, last_wrap]

    @pl.when(wraps[0] == 1)
    def _():
        for i in range(3):
            load(wrapped[i], spots[i], sems.at[i])

    @pl.when(wraps[0] == 0)
    def _():
        for i in range(3):
            load(inner[i], spots[i], sems.at[i])

    b_copy.wait()
    halve(b_in, right, 0, blocks)
    for i in range(3):
        pltpu.make_async_copy(wrapped[i], spots[i], sems.at[i]).wait()
        halve(a_in, left, i * third, third)
    c_copy.wait()
    multiply(1, idx_a, idx_b, idx_c, count, left, right, acc)
    out_copy = load(acc.at[pl.ds(0, blocks)], out_ref, sems.at[5])
    chosen = acc[diag[0, 0]]
    eye = lax.broadcasted_iota(jnp.int32, (BS, BS), 0) == lax.broadcasted_iota(jnp.int32, (BS, BS), 1)
    picked = jnp.where(eye, chosen, 0.0)
    trace_ref[...] = jnp.broadcast_to(jnp.sum(picked, keepdims=True), trace_ref.shape)
    out_copy.wait()


SMEM = pl.BlockSpec(memory_space=pltpu.SMEM)
HBM = pl.BlockSpec(memory_space=pl.ANY)


def scratch(blocks, sems):
    return [
        pltpu.VMEM((blocks, BS, BS), jnp.float32),
        pltpu.VMEM((blocks, BS, BS), jnp.float32),
        pltpu.VMEM((blocks, BS, 2 * BS), jnp.bfloat16),
        pltpu.VMEM((blocks, BS, 2 * BS), jnp.bfloat16),
        pltpu.VMEM((blocks + 1, BS, BS), jnp.float32),
        pltpu.SemaphoreType.DMA((sems,)),
    ]


def local(a_blocks, b_blocks, c_prior, pair_a, pair_b, pair_c, pair_count, diag_slot):
    blocks = a_blocks.shape[2]
    third = blocks // 3
    hop = lambda array, pairs: lax.ppermute(array, AXES, pairs)
    a = a_blocks[0, 0]
    stored = jax.ShapeDtypeStruct((blocks, BS, BS), jnp.float32)
    lists = (pair_a, pair_b, pair_c, pair_count)
    cost = pl.CostEstimate(flops=8 * 320 * BS**3, bytes_accessed=16 * MIB, transcendentals=0)
    params = pltpu.CompilerParams(vmem_limit_bytes=24 * MIB)

    first = hop(a[:third], RING)
    mid_relay = hop(a[third : 2 * third], TO_2)
    b_next = lax.ppermute(b_blocks, "row", ROWS)
    c_now = pl.pallas_call(
        first_kernel,
        in_specs=[SMEM] * 4 + [HBM] * 3,
        out_specs=HBM,
        out_shape=stored,
        scratch_shapes=scratch(blocks, 4),
        compiler_params=params,
        cost_estimate=cost,
        name="step0",
    )(*lists, a_blocks, b_blocks, c_prior)
    a_late, first, mid_relay, c_now = lax.optimization_barrier((a, first, mid_relay, c_now))
    first_wrap = hop(first, FROM_3)
    mid_wrap = hop(mid_relay, FROM_2)
    last_wrap = hop(a_late[2 * third :], DIRECT)
    rest = hop(a_late[third:], INNER)

    wraps = (lax.axis_index("col") % 4 == 3).astype(jnp.int32)[None]
    c_now, term = pl.pallas_call(
        second_kernel,
        in_specs=[SMEM] * 6 + [HBM] * 7,
        out_specs=[HBM, pl.BlockSpec(memory_space=pltpu.VMEM)],
        out_shape=[stored, jax.ShapeDtypeStruct((8, 128), jnp.float32)],
        scratch_shapes=scratch(blocks, 6),
        compiler_params=params,
        cost_estimate=cost,
        name="step1",
    )(*lists, diag_slot, wraps, first, first_wrap, rest, mid_wrap, last_wrap, b_next, c_now)
    devices = lax.axis_size(AXES)
    terms = lax.all_to_all(jnp.broadcast_to(term[:1, :1], (devices, 1)), AXES, 0, 0, tiled=True)
    trace_value = jnp.sum(terms) / (BS * jnp.sqrt(jnp.float32(devices)))
    return (c_now[None, None], trace_value)


def solution(mesh):
    wide, lists = P("row", "col", None, None, None), P("row", "col", None, None)
    placed = (wide, wide, wide, lists, lists, lists, P("row", "col", None), P("row", "col"))
    return jax.shard_map(local, mesh=mesh, in_specs=placed, out_specs=(wide, P()), check_vma=False)
```

time: 403 us -> 139 us (0.34)
  matrix products: 98.4 us -> 0 us
  other arithmetic: 90.3 us -> 0.87 us
  local copies, waits for them, and re-layouts: 94.3 us -> 11.2 us
  blocking collectives: 74.2 us -> 39.5 us
  waiting for transfers between devices: 26.3 us -> 41.9 us
  Pallas kernels: 0 us -> 14.2 us
  starting transfers between devices: 13.4 us -> 27.1 us
    dot_general x10 -> x0, matrix products: 98.4 us -> none  [one_group(): jnp.einsum('pij,pjk->pik', left_pick, right_pick, precision=lax.Precision...]
    gather x20 -> x0, local copies, waits for them, and re-layouts: 93 us -> none  [the longest x10 46.7 us: one_group(): right_pick = stores[0][1][gb]]
    scatter-add x10 -> x0, other arithmetic: 88 us -> none  [one_group(): return (total.at[gc].add(prod * gl[:, None, None]), None)]
    psum x1 -> x0, blocking collectives: 74.2 us -> none  [local(): total = lax.psum(local_trace, ('row', 'col'))]
    all_to_all x0 -> x1, blocking collectives: none -> 39.5 us  [local(): lax.all_to_all(jnp.broadcast_to(term[:1, :1], (devices, 1)), AXES, 0, 0,...]
    ppermute x2 -> x7, waiting for transfers between devices: 26.3 us -> 41.9 us  [the longest x6 41.9 us: local(): hop = lambda array, pairs: lax.ppermute(array, AXES, pairs)]
    pallas_call x0 -> x2, Pallas kernels: none -> 14.2 us  [the longest x1 8.53 us: local(): pl.pallas_call(second_kernel, in_specs=[SMEM] * 6 + [HBM] * 7, out_specs=...]
    ppermute x2 -> x7, starting transfers between devices: 13.4 us -> 27.1 us  [the longest x6 26.2 us: local(): hop = lambda array, pairs: lax.ppermute(array, AXES, pairs)]
  transfers between devices with their start and end apart: 2 -> 7, of which waited for: 1 -> 4; matrix products, arithmetic and copies ran while one was open for 36% -> 2% of each run, Pallas kernels for 0% -> 4%
where the time goes in v1:
time: 139 us; the launch traced here: 138 us
  waiting for transfers between devices  41.9 us (30%)
  blocking collectives  39.5 us (28%)
  starting transfers between devices  27.1 us (19%)
  Pallas kernels  14.2 us (10%)
  local copies, waits for them, and re-layouts  11.2 us (8%)
  between operations  3.18 us (2%)
    ppermute x6, waiting for transfers between devices, local(): hop = lambda array, pairs: lax.ppermute(array, AXES, pairs)  41.9 us
    all_to_all x1, blocking collectives, local(): lax.all_to_all(jnp.broadcast_to(term[:1, :1], (devices, 1)), AXES, 0, 0,...  39.5 us
    ppermute x6, starting transfers between devices, local(): hop = lambda array, pairs: lax.ppermute(array, AXES, pairs)  26.2 us
    pallas_call x1, Pallas kernels, local(): pl.pallas_call(second_kernel, in_specs=[SMEM] * 6 + [HBM] * 7, out_specs=...  8.53 us
    unnamed x18, local copies, waits for them, and re-layouts  5.69 us
    pallas_call x1, Pallas kernels, local(): pl.pallas_call(first_kernel, in_specs=[SMEM] * 4 + [HBM] * 3, out_specs=H...  5.62 us
  transfers between devices with their start and end apart: 7, of which 4 were waited for; matrix products, arithmetic and copies ran while one was open for 2% of the time, Pallas kernels for 4%

profile of v1, /device:TPU:1, one launch (start us, length us, event | category | flops | bytes accessed | tf_op | source)
XLA Modules:
  0.0 138.0 jit_solution(933762389685830841)
XLA Ops:
  0.6 0.0 copy-start
  0.6 0.0 copy-start.6
  0.7 0.0 copy-start.5
  0.7 0.0 copy-start.4
  0.7 0.0 copy-start.3
  0.7 1.8 %slice_bitcast_fusion = (f32[16,128,128]{2,1,0:T(8,128)S(1)}, f32[16,128,128]{2,1,0:T(8,128)S(1)}) fusion(f32[1,1,48,128,128]{4,3,2,1,0:T(8,128)} %a_ref.1), kind=kLoop, calls=%fused_computation | loop fusion | bytes 4194304 | tf_op jit(solution)/shard_map/slice | solution.py:169
  2.5 8.9 %collective-permute-start.1 = (f32[16,128,128]{2,1,0:T(8,128)S(1)}, f32[16,128,128]{2,1,0:T(8,128)}, u32[]{:S(2)}, u32[]{:S(2)}) collective-permute-start(f32[16,128,128]{2,1,0:T(8,128)S(1)} %get-tuple-element.14), channel_id=1, source_target_pairs={{0,26},{4,6},{8,2},{12,14},{16,10},{20,22},{24,18},{28,30},{32,58}... | collective-permute-start | bytes 3145736 | tf_op jit(solution)/shard_map/ppermute | solution.py:161
  11.5 0.0 collective-permute-start
  11.5 1.0 collective-permute-start.6
  12.4 0.0 copy-done
  12.4 0.0 copy-done.6
  12.4 0.0 copy-done.5
  12.4 0.0 copy-done.4
  12.4 0.0 copy-done.3
  12.4 0.0 copy-start.1
  12.5 1.9 %copy-done.1 = f32[1,1,48,128,128]{4,3,2,1,0:T(8,128)S(1)} copy-done((f32[1,1,48,128,128]{4,3,2,1,0:T(8,128)S(1)}, f32[1,1,48,128,128]{4,3,2,1,0:T(8,128)}, u32[]{:S(2)}) %copy-start.1) | copy-done | bytes 3145752
  14.3 0.0 copy-start.2
  14.3 1.9 %copy-done.2 = f32[1,1,48,128,128]{4,3,2,1,0:T(8,128)S(1)} copy-done((f32[1,1,48,128,128]{4,3,2,1,0:T(8,128)S(1)}, f32[1,1,48,128,128]{4,3,2,1,0:T(8,128)}, u32[]{:S(2)}) %copy-start.2) | copy-done | bytes 3145752
  16.2 5.6 %step0.1.c_ref = f32[48,128,128]{2,1,0:T(8,128)S(1)} custom-call(s32[1,1,2,320]{3,2,1,0:T(2,128)S(1)} %copy-done.3, s32[1,1,2,320]{3,2,1,0:T(2,128)S(1)} %copy-done.4, s32[1,1,2,320]{3,2,1,0:T(2,128)S(1)} %copy-done.5, s32[1,1,2]{2,1,0:T(1,128)S(1)} %copy-done.6, f32[1,1,48,128,128]{4,3,2,1,0:T(8,128)S(1)} %copy-done, f32[1,1,48,128,128]{4,3,2,1,0:T(8,128)S(1)} %copy-done.2, ...), custom_call_target="tpu_custom_call" | custom-call | flops 5368709120 | bytes 16777216 | tf_op jit(solution)/shard_map/step0/pallas_call | solution.py:171
  21.9 0.0 copy-start.7
  21.9 10.4 %collective-permute-done.1 = f32[16,128,128]{2,1,0:T(8,128)} collective-permute-done((f32[16,128,128]{2,1,0:T(8,128)S(1)}, f32[16,128,128]{2,1,0:T(8,128)}, u32[]{:S(2)}, u32[]{:S(2)}) %collective-permute-start.1) | collective-permute-done | bytes 1048608 | tf_op jit(solution)/shard_map/ppermute | solution.py:161
  32.3 3.0 %collective-permute-done.first_in = f32[16,128,128]{2,1,0:T(8,128)} collective-permute-done((f32[16,128,128]{2,1,0:T(8,128)S(1)}, f32[16,128,128]{2,1,0:T(8,128)}, u32[]{:S(2)}, u32[]{:S(2)}) %collective-permute-start) | collective-permute-done | bytes 1048608 | tf_op jit(solution)/shard_map/ppermute | solution.py:161
  35.3 1.5 %slice.25 = f32[32,128,128]{2,1,0:T(8,128)} slice(f32[48,128,128]{2,1,0:T(8,128)S(1)} %bitcast.8), slice={[16:48], [0:128], [0:128]} | slice | bytes 4194304 | tf_op jit(solution)/shard_map/slice | solution.py:185
  36.7 1.3 collective-permute-start.3
  38.0 1.0 slice.26
  39.1 0.0 copy-done.7
  39.1 12.6 %collective-permute-start.5 = (f32[16,128,128]{2,1,0:T(8,128)}, f32[16,128,128]{2,1,0:T(8,128)}, u32[]{:S(2)}, u32[]{:S(2)}) collective-permute-start(f32[16,128,128]{2,1,0:T(8,128)} %slice.26), channel_id=1, source_target_pairs={{0,31},{4,3},{8,7},{12,11},{16,15},{20,19},{24,23},{28,27},{32,63}... | collective-permute-start | bytes 3145736 | tf_op jit(solution)/shard_map/ppermute | solution.py:161
  51.7 1.7 %collective-permute-start.4 = (f32[16,128,128]{2,1,0:T(8,128)}, f32[16,128,128]{2,1,0:T(8,128)}, u32[]{:S(2)}, u32[]{:S(2)}) collective-permute-start(f32[16,128,128]{2,1,0:T(8,128)} %collective-permute-done.1), channel_id=1, source_target_pairs={{2,7},{6,3},{10,15},{14,11},{18,23},{22,19},{26,31},{30,27},{34,39... | collective-permute-start | bytes 3145736 | tf_op jit(solution)/shard_map/ppermute | solution.py:161
  53.4 1.7 %collective-permute-start.2 = (f32[16,128,128]{2,1,0:T(8,128)}, f32[16,128,128]{2,1,0:T(8,128)}, u32[]{:S(2)}, u32[]{:S(2)}) collective-permute-start(f32[16,128,128]{2,1,0:T(8,128)} %collective-permute-done.first_in), channel_id=1, source_target_pairs={{3,7},{7,3},{11,15},{15,11},{19,23},{23,19},{27,31},{31,27},{35,39... | collective-permute-start | bytes 3145736 | tf_op jit(solution)/shard_map/ppermute | solution.py:161
  55.7 17.3 %collective-permute-done.5.last_wrap = f32[16,128,128]{2,1,0:T(8,128)} collective-permute-done((f32[16,128,128]{2,1,0:T(8,128)}, f32[16,128,128]{2,1,0:T(8,128)}, u32[]{:S(2)}, u32[]{:S(2)}) %collective-permute-start.5) | collective-permute-done | bytes 1048608 | tf_op jit(solution)/shard_map/ppermute | solution.py:161
  73.0 0.0 collective-permute-done.4.mid_wrap
  73.0 0.0 collective-permute-done.2.first_wrap
  73.0 11.2 %collective-permute-done.3.rest_in = f32[32,128,128]{2,1,0:T(8,128)} collective-permute-done((f32[32,128,128]{2,1,0:T(8,128)}, f32[32,128,128]{2,1,0:T(8,128)}, u32[]{:S(2)}, u32[]{:S(2)}) %collective-permute-start.3) | collective-permute-done | bytes 2097184 | tf_op jit(solution)/shard_map/ppermute | solution.py:161
  84.2 0.0 collective-permute-done.6.b_ref
  84.2 0.0 copy-start.8
  84.2 1.9 %copy-done.8 = f32[48,128,128]{2,1,0:T(8,128)S(1)} copy-done((f32[48,128,128]{2,1,0:T(8,128)S(1)}, f32[48,128,128]{2,1,0:T(8,128)}, u32[]{:S(2)}) %copy-start.8) | copy-done | bytes 3145752
  86.1 8.5 %step1.1 = (f32[48,128,128]{2,1,0:T(8,128)}, f32[8,128]{1,0:T(8,128)S(1)}) custom-call(s32[1,1,2,320]{3,2,1,0:T(2,128)S(1)} %copy-done.3, s32[1,1,2,320]{3,2,1,0:T(2,128)S(1)} %copy-done.4, s32[1,1,2,320]{3,2,1,0:T(2,128)S(1)} %copy-done.5, s32[1,1,2]{2,1,0:T(1,128)S(1)} %copy-done.6, s32[1,1]{1,0:T(1,128)S(6)} %copy.12.diag, s32[1]{0:T(128)} %bitcast.wraps, ...), custom_call_target="tpu_custom_call" | custom-call | flops 5368709120 | bytes 16777216 | tf_op jit(solution)/shard_map/step1/pallas_call | solution.py:188
  94.6 0.5 slice.27
  95.1 0.7 broadcast_in_dim.19
  95.9 39.5 %all_to_all.6 = f32[256,1,1]{2,1,0:T(1,128)S(1)} all-to-all(f32[256,1,1]{2,1,0:T(1,128)S(1)} %broadcast_in_dim.19), channel_id=1, replica_groups=mesh['row'=8,'col'=32] {'row','col'}, dimensions={0} | all-to-all | bytes 2048 | tf_op jit(solution)/shard_map/all_to_all | solution.py:199
  135.4 0.9 reduce_sum.9
Async XLA Ops:
  0.6 11.8 %copy-start = (f32[1,1,48,128,128]{4,3,2,1,0:T(8,128)S(1)}, f32[1,1,48,128,128]{4,3,2,1,0:T(8,128)}, u32[]{:S(2)}) copy-start(f32[1,1,48,128,128]{4,3,2,1,0:T(8,128)} %a_ref.1) | copy-start | bytes 9437188
  0.6 11.8 %copy-start.6 = (s32[1,1,2]{2,1,0:T(1,128)S(1)}, s32[1,1,2]{2,1,0:T(1,128)}, u32[]{:S(2)}) copy-start(s32[1,1,2]{2,1,0:T(1,128)} %count.3) | copy-start | bytes 28
  0.7 11.8 %copy-start.5 = (s32[1,1,2,320]{3,2,1,0:T(2,128)S(1)}, s32[1,1,2,320]{3,2,1,0:T(2,128)}, u32[]{:S(2)}) copy-start(s32[1,1,2,320]{3,2,1,0:T(2,128)} %idx_c.3) | copy-start | bytes 7684
  0.7 11.8 %copy-start.4 = (s32[1,1,2,320]{3,2,1,0:T(2,128)S(1)}, s32[1,1,2,320]{3,2,1,0:T(2,128)}, u32[]{:S(2)}) copy-start(s32[1,1,2,320]{3,2,1,0:T(2,128)} %idx_b.3) | copy-start | bytes 7684
  0.7 11.8 %copy-start.3 = (s32[1,1,2,320]{3,2,1,0:T(2,128)S(1)}, s32[1,1,2,320]{3,2,1,0:T(2,128)}, u32[]{:S(2)}) copy-start(s32[1,1,2,320]{3,2,1,0:T(2,128)} %idx_a.3) | copy-start | bytes 7684
  2.5 29.7 %collective-permute-start.1 = (f32[16,128,128]{2,1,0:T(8,128)S(1)}, f32[16,128,128]{2,1,0:T(8,128)}, u32[]{:S(2)}, u32[]{:S(2)}) collective-permute-start(f32[16,128,128]{2,1,0:T(8,128)S(1)} %get-tuple-element.14), channel_id=1, source_target_pairs={{0,26},{4,6},{8,2},{12,14},{16,10},{20,22},{24,18},{28,30},{32,58}... | collective-permute-start | bytes 3145736 | tf_op jit(solution)/shard_map/ppermute | solution.py:161
  11.5 23.8 %collective-permute-start = (f32[16,128,128]{2,1,0:T(8,128)S(1)}, f32[16,128,128]{2,1,0:T(8,128)}, u32[]{:S(2)}, u32[]{:S(2)}) collective-permute-start(f32[16,128,128]{2,1,0:T(8,128)S(1)} %get-tuple-element.15), channel_id=1, source_target_pairs={{1,0},{2,1},{3,2},{5,4},{6,5},{7,6},{9,8},{10,9},{11,10},{13,12},{... | collective-permute-start | bytes 3145736 | tf_op jit(solution)/shard_map/ppermute | solution.py:161
  11.5 72.7 %collective-permute-start.6 = (f32[1,1,48,128,128]{4,3,2,1,0:T(8,128)}, f32[1,1,48,128,128]{4,3,2,1,0:T(8,128)S(1)}, u32[]{:S(2)}, u32[]{:S(2)}) collective-permute-start(f32[1,1,48,128,128]{4,3,2,1,0:T(8,128)} %b_ref.1), channel_id=1, source_target_pairs={{32,0},{64,32},{96,64},{128,96},{160,128},{192,160},{224,192},{0,2... | collective-permute-start | bytes 9437192 | tf_op jit(solution)/shard_map/ppermute | solution.py:170
  12.4 1.9 %copy-start.1 = (f32[1,1,48,128,128]{4,3,2,1,0:T(8,128)S(1)}, f32[1,1,48,128,128]{4,3,2,1,0:T(8,128)}, u32[]{:S(2)}) copy-start(f32[1,1,48,128,128]{4,3,2,1,0:T(8,128)} %c_ref.1) | copy-start | bytes 9437188
  14.3 1.9 %copy-start.2 = (f32[1,1,48,128,128]{4,3,2,1,0:T(8,128)S(1)}, f32[1,1,48,128,128]{4,3,2,1,0:T(8,128)}, u32[]{:S(2)}) copy-start(f32[1,1,48,128,128]{4,3,2,1,0:T(8,128)} %b_ref.1) | copy-start | bytes 9437188
  21.9 17.2 %copy-start.7 = (f32[48,128,128]{2,1,0:T(8,128)}, f32[48,128,128]{2,1,0:T(8,128)S(1)}, u32[]{:S(2)}) copy-start(f32[48,128,128]{2,1,0:T(8,128)S(1)} %step0.1.c_ref) | copy-start | bytes 9437188
  36.7 47.5 %collective-permute-start.3 = (f32[32,128,128]{2,1,0:T(8,128)}, f32[32,128,128]{2,1,0:T(8,128)}, u32[]{:S(2)}, u32[]{:S(2)}) collective-permute-start(f32[32,128,128]{2,1,0:T(8,128)} %slice.25), channel_id=1, source_target_pairs={{1,0},{2,1},{3,2},{5,4},{6,5},{7,6},{9,8},{10,9},{11,10},{13,12},{... | collective-permute-start | bytes 6291464 | tf_op jit(solution)/shard_map/ppermute | solution.py:161
  39.1 34.0 %collective-permute-start.5 = (f32[16,128,128]{2,1,0:T(8,128)}, f32[16,128,128]{2,1,0:T(8,128)}, u32[]{:S(2)}, u32[]{:S(2)}) collective-permute-start(f32[16,128,128]{2,1,0:T(8,128)} %slice.26), channel_id=1, source_target_pairs={{0,31},{4,3},{8,7},{12,11},{16,15},{20,19},{24,23},{28,27},{32,63}... | collective-permute-start | bytes 3145736 | tf_op jit(solution)/shard_map/ppermute | solution.py:161
  51.7 21.3 %collective-permute-start.4 = (f32[16,128,128]{2,1,0:T(8,128)}, f32[16,128,128]{2,1,0:T(8,128)}, u32[]{:S(2)}, u32[]{:S(2)}) collective-permute-start(f32[16,128,128]{2,1,0:T(8,128)} %collective-permute-done.1), channel_id=1, source_target_pairs={{2,7},{6,3},{10,15},{14,11},{18,23},{22,19},{26,31},{30,27},{34,39... | collective-permute-start | bytes 3145736 | tf_op jit(solution)/shard_map/ppermute | solution.py:161
  53.4 19.7 %collective-permute-start.2 = (f32[16,128,128]{2,1,0:T(8,128)}, f32[16,128,128]{2,1,0:T(8,128)}, u32[]{:S(2)}, u32[]{:S(2)}) collective-permute-start(f32[16,128,128]{2,1,0:T(8,128)} %collective-permute-done.first_in), channel_id=1, source_target_pairs={{3,7},{7,3},{11,15},{15,11},{19,23},{23,19},{27,31},{31,27},{35,39... | collective-permute-start | bytes 3145736 | tf_op jit(solution)/shard_map/ppermute | solution.py:161
  84.2 1.9 %copy-start.8 = (f32[48,128,128]{2,1,0:T(8,128)S(1)}, f32[48,128,128]{2,1,0:T(8,128)}, u32[]{:S(2)}) copy-start(f32[48,128,128]{2,1,0:T(8,128)} %copy-done.7) | copy-start | bytes 9437188

commit v2 on v1

v2 whole, which is shorter than its diff:
```python
import jax
import jax.numpy as jnp
from jax import lax
from jax.experimental import pallas as pl
from jax.experimental.pallas import tpu as pltpu
from jax.sharding import PartitionSpec as P

AXES = ("row", "col")
BS = 128
UNROLL = 64
BATCH = 16
PARTS = (15, 17, 16)
FIRST = (0, PARTS[0], PARTS[0] + PARTS[1])
MIB = 2**20


def coords(device):
    row, col = divmod(device, 32)
    z_lo, core = divmod(row, 2)
    y, low = divmod(col, 8)
    z_hi, x = divmod(low, 4)
    return x, y, z_hi * 4 + z_lo, core


def device_at(x, y, z, core):
    x, y, z = x % 4, y % 4, z % 8
    return ((z % 4) * 2 + core) * 32 + (y * 2 + z // 4) * 4 + x


def route(chosen, move):
    pairs = []
    for device in range(256):
        place = coords(device)
        if chosen(*place):
            pairs.append((device, device_at(*move(*place))))
    return pairs


def y_of(y, z):
    return y if z >= 4 else y - 1


INNER = route(lambda x, y, z, k: x >= 1, lambda x, y, z, k: (x - 1, y, z, k))
TO_3 = route(lambda x, y, z, k: x == 0, lambda x, y, z, k: (3, y_of(y, z), z, k))
TO_2 = route(lambda x, y, z, k: x == 0, lambda x, y, z, k: (2, y_of(y, z), z, k))
DIRECT = route(lambda x, y, z, k: x == 0, lambda x, y, z, k: (3, y_of(y, z), z + 4, k))
FROM_2 = route(lambda x, y, z, k: x == 2, lambda x, y, z, k: (3, y, z + 4, k))
FROM_3 = route(lambda x, y, z, k: x == 3, lambda x, y, z, k: (3, y, z + 4, k))
ROWS = [((i + 1) % 8, i) for i in range(8)]


def split(value):
    high = value.astype(jnp.bfloat16)
    return high, (value - high.astype(jnp.float32)).astype(jnp.bfloat16)


def multiply(step, idx_a, idx_b, idx_c, count, left, right, acc):
    live = count[0, 0, step]

    def product(pair):
        halves = left[idx_a[0, 0, step, pair]]
        weights = right[idx_b[0, 0, step, pair]]
        both = jnp.dot(halves, jnp.concatenate([weights, weights], axis=0), preferred_element_type=jnp.float32)
        return both[:, :BS] + both[:, BS:]

    def group(g, carry):
        for u in range(UNROLL):
            pair = g * UNROLL + u
            slot = jnp.where(pair < live, idx_c[0, 0, step, pair], acc.shape[0] - 1)
            acc[slot] = acc[slot] + product(pair)
        return carry

    lax.fori_loop(0, lax.div(live + UNROLL - 1, UNROLL), group, 0)


def load(source, target, sem):
    copy = pltpu.make_async_copy(source, target, sem)
    copy.start()
    return copy


def halve(source, target, start, size):
    def one(i):
        high, low = split(source[i])
        target[i, :, 0:BS] = high
        target[i, :, BS:] = low

    def four(g, carry):
        for u in range(4):
            one(start + g * 4 + u)
        return carry

    lax.fori_loop(0, size // 4, four, 0)
    for i in range(size // 4 * 4, size):
        one(start + i)


def first_kernel(idx_a, idx_b, idx_c, count, a_ref, b_ref, c_ref, out_ref, a_in, b_in, left, right, acc, sems):
    blocks = a_in.shape[0]
    copies = [
        load(a_ref.at[0, 0], a_in, sems.at[0]),
        load(b_ref.at[0, 0], b_in, sems.at[1]),
        load(c_ref.at[0, 0], acc.at[pl.ds(0, blocks)], sems.at[2]),
    ]
    copies[0].wait()
    halve(a_in, left, 0, blocks)
    copies[1].wait()
    halve(b_in, right, 0, blocks)
    copies[2].wait()
    multiply(0, idx_a, idx_b, idx_c, count, left, right, acc)
    load(acc.at[pl.ds(0, blocks)], out_ref, sems.at[3]).wait()


def halve_kernel(idx_a, idx_b, idx_c, count, diag, source, target, listing, staged, sem):
    copy = load(source.at[0, 0], staged, sem)

    def collect(pair, found):
        listing[0, found] = idx_a[0, 0, 1, pair]
        listing[1, found] = idx_b[0, 0, 1, pair]
        return found + (idx_c[0, 0, 1, pair] == diag[0, 0]).astype(jnp.int32)

    found = lax.fori_loop(0, count[0, 0, 1], collect, 0)
    for i in range(BATCH):
        listing[0, found + i] = 0
        listing[1, found + i] = 0
    listing[2, 0] = found
    copy.wait()
    halve(staged, target, 0, staged.shape[0])


def second_kernel(
    idx_a, idx_b, idx_c, count, wraps,
    inner, last_wrap, mid_wrap, first_wrap, right, c_ref,
    out_ref, acc, a_in, left, sems,
):
    blocks = a_in.shape[0]
    spots = [a_in.at[pl.ds(at, size)] for at, size in zip(FIRST, PARTS)]
    wrapped = [first_wrap, mid_wrap, last_wrap]

    @pl.when(wraps[0] == 1)
    def _():
        for i in range(3):
            load(wrapped[i], spots[i], sems.at[i])

    @pl.when(wraps[0] == 0)
    def _():
        for i in range(3):
            load(inner.at[0, 0, pl.ds(FIRST[i], PARTS[i])], spots[i], sems.at[i])

    c_copy = load(c_ref, acc.at[pl.ds(0, blocks)], sems.at[4])
    for i in range(3):
        pltpu.make_async_copy(wrapped[i], spots[i], sems.at[i]).wait()
        halve(a_in, left, FIRST[i], PARTS[i])
    c_copy.wait()
    multiply(1, idx_a, idx_b, idx_c, count, left, right, acc)
    load(acc.at[pl.ds(0, blocks)], out_ref, sems.at[3]).wait()


def trace_kernel(
    listing, diag, wraps, inner, last_wrap, mid_wrap, first_wrap, right, c_ref, term_ref, a_in, total, sem, c_sem
):
    found = listing[2, 0]
    load(c_ref.at[diag[0, 0]], total, c_sem).wait()
    parts = [first_wrap, mid_wrap, last_wrap]

    def batch(g, carry):
        for i in range(BATCH):
            block = listing[0, g * BATCH + i]
            part = (block >= FIRST[1]).astype(jnp.int32) + (block >= FIRST[2]).astype(jnp.int32)

            @pl.when(wraps[0] == 0)
            def _():
                load(inner.at[0, 0, block], a_in.at[i], sem)

            for j in range(3):

                @pl.when(jnp.logical_and(wraps[0] == 1, part == j))
                def _():
                    load(parts[j].at[block - FIRST[j]], a_in.at[i], sem)

        pltpu.make_async_copy(inner.at[0, 0, pl.ds(0, BATCH)], a_in, sem).wait()
        for i in range(BATCH):
            halves_of = jnp.concatenate(split(a_in[i]), axis=1)
            weights = right[listing[1, g * BATCH + i]]
            both = jnp.dot(halves_of, jnp.concatenate([weights, weights], axis=0), preferred_element_type=jnp.float32)
            total[...] += jnp.where(g * BATCH + i < found, both[:, :BS] + both[:, BS:], 0.0)
        return carry

    lax.fori_loop(0, lax.div(found + BATCH - 1, BATCH), batch, 0)
    eye = lax.broadcasted_iota(jnp.int32, (BS, BS), 0) == lax.broadcasted_iota(jnp.int32, (BS, BS), 1)
    picked = jnp.where(eye, total[...], 0.0)
    term_ref[...] = jnp.broadcast_to(jnp.sum(picked, keepdims=True), term_ref.shape)


SMEM = pl.BlockSpec(memory_space=pltpu.SMEM)
VMEM = pl.BlockSpec(memory_space=pltpu.VMEM)
HBM = pl.BlockSpec(memory_space=pl.ANY)


def behind_kernel(first_ref, mid_ref, token_ref):
    token_ref[0, 0] = 0


def behind(*arrays):
    return pl.pallas_call(
        behind_kernel,
        in_specs=[HBM] * len(arrays),
        out_specs=SMEM,
        out_shape=jax.ShapeDtypeStruct((1, 1), jnp.int32),
        compiler_params=pltpu.CompilerParams(vmem_limit_bytes=24 * MIB),
        cost_estimate=pl.CostEstimate(flops=0, bytes_accessed=4 * MIB, transcendentals=0),
        name="behind",
    )(*arrays)


def local(a_blocks, b_blocks, c_prior, pair_a, pair_b, pair_c, pair_count, diag_slot):
    blocks = a_blocks.shape[2]
    devices = lax.axis_size(AXES)
    hop = lambda array, pairs: lax.ppermute(array, AXES, pairs)
    a = a_blocks[0, 0]
    lists = (pair_a, pair_b, pair_c, pair_count)
    whole = (blocks, BS, BS)
    wide, padded = (blocks, BS, 2 * BS), (blocks + 1, BS, BS)
    cost = pl.CostEstimate(flops=8 * 320 * BS**3, bytes_accessed=16 * MIB, transcendentals=0)
    params = pltpu.CompilerParams(vmem_limit_bytes=56 * MIB)

    a_first, a_mid = a[: FIRST[1]], a[FIRST[1] : FIRST[2]]
    first_relay = hop(a_first, TO_3)
    mid_relay = hop(a_mid, TO_2)
    a_inner, b_sent, token = lax.optimization_barrier((a_blocks, b_blocks, behind(a_first, a_mid)))
    inner = hop(a_inner, INNER)
    b_next = lax.ppermute(b_sent, "row", ROWS)
    c_now = pl.pallas_call(
        first_kernel,
        in_specs=[SMEM] * 4 + [HBM] * 3,
        out_specs=HBM,
        out_shape=jax.ShapeDtypeStruct(whole, jnp.float32),
        scratch_shapes=[
            pltpu.VMEM(whole, jnp.float32),
            pltpu.VMEM(whole, jnp.float32),
            pltpu.VMEM(wide, jnp.bfloat16),
            pltpu.VMEM(wide, jnp.bfloat16),
            pltpu.VMEM(padded, jnp.float32),
            pltpu.SemaphoreType.DMA((4,)),
        ],
        compiler_params=params,
        cost_estimate=cost,
        name="step0",
    )(*lists, a_blocks, b_blocks, c_prior)
    a_last, mid_relay, c_now = lax.optimization_barrier((a_inner[0, 0, FIRST[2] :], mid_relay, c_now))
    last_wrap = hop(a_last, DIRECT)
    mid_wrap = hop(mid_relay, FROM_2)
    first_wrap = hop(first_relay, FROM_3)
    right, listing = pl.pallas_call(
        halve_kernel,
        in_specs=[SMEM] * 5 + [HBM],
        out_specs=[VMEM, SMEM],
        out_shape=[pltpu.VMEM(wide, jnp.bfloat16), jax.ShapeDtypeStruct((3, 384), jnp.int32)],
        scratch_shapes=[pltpu.VMEM(whole, jnp.float32), pltpu.SemaphoreType.DMA],
        compiler_params=params,
        cost_estimate=pl.CostEstimate(flops=MIB, bytes_accessed=6 * MIB, transcendentals=0),
        name="halves",
    )(*lists, diag_slot, b_next)

    wraps = (lax.axis_index("col") % 4 == 3).astype(jnp.int32)[None]
    wraps, last_wrap, mid_wrap, right = lax.optimization_barrier((wraps + token[0, :1], last_wrap, mid_wrap, right))
    term = pl.pallas_call(
        trace_kernel,
        in_specs=[SMEM] * 3 + [HBM] * 4 + [VMEM, HBM],
        out_specs=VMEM,
        out_shape=jax.ShapeDtypeStruct((devices, BS), jnp.float32),
        scratch_shapes=[
            pltpu.VMEM((BATCH, BS, BS), jnp.float32),
            pltpu.VMEM((BS, BS), jnp.float32),
            pltpu.SemaphoreType.DMA,
            pltpu.SemaphoreType.DMA,
        ],
        compiler_params=params,
        cost_estimate=pl.CostEstimate(flops=8 * BATCH * BS**3, bytes_accessed=MIB, transcendentals=0),
        name="trace_term",
    )(listing, diag_slot, wraps, inner, last_wrap, mid_wrap, first_wrap, right, c_now)
    terms = lax.all_to_all(term, AXES, 0, 0, tiled=True)
    c_now = pl.pallas_call(
        second_kernel,
        in_specs=[SMEM] * 5 + [HBM] * 4 + [VMEM, HBM],
        out_specs=HBM,
        out_shape=jax.ShapeDtypeStruct(whole, jnp.float32),
        scratch_shapes=[
            pltpu.VMEM(padded, jnp.float32),
            pltpu.VMEM(whole, jnp.float32),
            pltpu.VMEM(wide, jnp.bfloat16),
            pltpu.SemaphoreType.DMA((5,)),
        ],
        compiler_params=params,
        cost_estimate=cost,
        name="step1",
    )(*lists, wraps, inner, last_wrap, mid_wrap, first_wrap, right, c_now)
    trace_value = jnp.sum(terms[:, 0]) / (BS * jnp.sqrt(jnp.float32(devices)))
    return (c_now[None, None], trace_value)


def solution(mesh):
    wide, lists = P("row", "col", None, None, None), P("row", "col", None, None)
    placed = (wide, wide, wide, lists, lists, lists, P("row", "col", None), P("row", "col"))
    return jax.shard_map(local, mesh=mesh, in_specs=placed, out_specs=(wide, P()), check_vma=False)
```

time: 139 us -> 128 us (0.921)
  blocking collectives: 39.5 us -> 0 us
  starting transfers between devices: 27.1 us -> 53.7 us
  Pallas kernels: 14.2 us -> 32.2 us
  waiting for transfers between devices: 41.9 us -> 31.6 us
  local copies, waits for them, and re-layouts: 11.2 us -> 5.55 us
    all_to_all x1 -> x0, blocking collectives: 39.5 us -> none  [local(): lax.all_to_all(jnp.broadcast_to(term[:1, :1], (devices, 1)), AXES, 0, 0,...]
    all_to_all x0 -> x1, starting transfers between devices: none -> 30.3 us  [local(): terms = lax.all_to_all(term, AXES, 0, 0, tiled=True)]
    pallas_call x1 -> x4, Pallas kernels: 8.53 us -> 23.4 us  [the longest x1 12.9 us: local(): pl.pallas_call(second_kernel, in_specs=[SMEM] * 5 + [HBM] * 4 + [VMEM, HB...]
    ppermute x6, waiting for transfers between devices: 41.9 us -> 31.6 us  [local(): hop = lambda array, pairs: lax.ppermute(array, AXES, pairs)]
    ppermute x6, starting transfers between devices: 26.2 us -> 20.1 us  [local(): hop = lambda array, pairs: lax.ppermute(array, AXES, pairs)]
    unnamed x18 -> x4, local copies, waits for them, and re-layouts: 5.69 us -> 1.7 us
    pallas_call x1, Pallas kernels: 5.62 us -> 8.87 us  [local(): pl.pallas_call(first_kernel, in_specs=[SMEM] * 4 + [HBM] * 3, out_specs=H...]
    ppermute x1, starting transfers between devices: 0.96 us -> 3.32 us  [local(): b_next = lax.ppermute(b_sent, 'row', ROWS)]
  transfers between devices with their start and end apart: 7 -> 8, of which waited for: 4 -> 3; matrix products, arithmetic and copies ran while one was open for 2% -> 1% of each run, Pallas kernels for 4% -> 21%
where the time goes in v2:
time: 128 us
  starting transfers between devices  53.7 us (42%)
  Pallas kernels  32.2 us (25%)
  waiting for transfers between devices  31.6 us (25%)
  local copies, waits for them, and re-layouts  5.55 us (4%)
  between operations  3.86 us (3%)
    ppermute x6, waiting for transfers between devices, local(): hop = lambda array, pairs: lax.ppermute(array, AXES, pairs)  31.6 us
    all_to_all x1, starting transfers between devices, local(): terms = lax.all_to_all(term, AXES, 0, 0, tiled=True)  30.3 us
    ppermute x6, starting transfers between devices, local(): hop = lambda array, pairs: lax.ppermute(array, AXES, pairs)  20.1 us
    pallas_call x1, Pallas kernels, local(): pl.pallas_call(second_kernel, in_specs=[SMEM] * 5 + [HBM] * 4 + [VMEM, HB...  12.9 us
    pallas_call x1, Pallas kernels, local(): pl.pallas_call(first_kernel, in_specs=[SMEM] * 4 + [HBM] * 3, out_specs=H...  8.87 us
    pallas_call x1, Pallas kernels, local(): pl.pallas_call(trace_kernel, in_specs=[SMEM] * 3 + [HBM] * 4 + [VMEM, HBM...  5.51 us
    pallas_call x1, Pallas kernels, local(): pl.pallas_call(halve_kernel, in_specs=[SMEM] * 5 + [HBM], out_specs=[VMEM...  4.49 us
    ppermute x1, starting transfers between devices, local(): b_next = lax.ppermute(b_sent, 'row', ROWS)  3.32 us
  transfers between devices with their start and end apart: 8, of which 3 were waited for; matrix products, arithmetic and copies ran while one was open for 1% of the time, Pallas kernels for 21%

profile of v2, /device:TPU:1, one launch (start us, length us, event | category | flops | bytes accessed | tf_op | source)
XLA Modules:
  0.0 127.6 jit_solution(14472847855795611447)
XLA Ops:
  0.6 0.0 copy-start.1
  0.6 1.5 %slice_bitcast_fusion.mid_ref = f32[17,128,128]{2,1,0:T(8,128)S(1)} fusion(f32[1,1,48,128,128]{4,3,2,1,0:T(8,128)} %a_ref.1), kind=kLoop, calls=%fused_computation | loop fusion | bytes 2228224 | tf_op jit(solution)/shard_map/slice | solution.py:227
  2.1 1.3 %slice_bitcast_fusion.2.first_ref = f32[15,128,128]{2,1,0:T(8,128)S(1)} fusion(f32[1,1,48,128,128]{4,3,2,1,0:T(8,128)} %a_ref.1), kind=kLoop, calls=%fused_computation.2 | loop fusion | bytes 1966080 | tf_op jit(solution)/shard_map/slice | solution.py:227
  3.4 0.5 behind.1
  4.0 3.3 %collective-permute-start.3 = (f32[1,1,48,128,128]{4,3,2,1,0:T(8,128)}, f32[1,1,48,128,128]{4,3,2,1,0:T(8,128)}, u32[]{:S(2)}, u32[]{:S(2)}) collective-permute-start(f32[1,1,48,128,128]{4,3,2,1,0:T(8,128)} %b_ref.1), channel_id=1, source_target_pairs={{32,0},{64,32},{96,64},{128,96},{160,128},{192,160},{224,192},{0,2... | collective-permute-start | bytes 9437192 | tf_op jit(solution)/shard_map/ppermute | solution.py:232
  7.3 0.0 copy-done.1
  7.3 1.3 %collective-permute-start.4 = (f32[1,1,48,128,128]{4,3,2,1,0:T(8,128)S(1)}, f32[1,1,48,128,128]{4,3,2,1,0:T(8,128)}, u32[]{:S(2)}, u32[]{:S(2)}) collective-permute-start(f32[1,1,48,128,128]{4,3,2,1,0:T(8,128)S(1)} %copy-done.1), channel_id=1, source_target_pairs={{1,0},{2,1},{3,2},{5,4},{6,5},{7,6},{9,8},{10,9},{11,10},{13,12},{... | collective-permute-start | bytes 9437192 | tf_op jit(solution)/shard_map/ppermute | solution.py:219
  8.6 7.3 %collective-permute-start = (f32[17,128,128]{2,1,0:T(8,128)S(1)}, f32[17,128,128]{2,1,0:T(8,128)}, u32[]{:S(2)}, u32[]{:S(2)}) collective-permute-start(f32[17,128,128]{2,1,0:T(8,128)S(1)} %slice_bitcast_fusion.mid_ref), channel_id=1, source_target_pairs={{0,26},{4,6},{8,2},{12,14},{16,10},{20,22},{24,18},{28,30},{32,58}... | collective-permute-start | bytes 3342344 | tf_op jit(solution)/shard_map/ppermute | solution.py:219
  15.8 3.3 %collective-permute-start.5 = (f32[15,128,128]{2,1,0:T(8,128)S(1)}, f32[15,128,128]{2,1,0:T(8,128)}, u32[]{:S(2)}, u32[]{:S(2)}) collective-permute-start(f32[15,128,128]{2,1,0:T(8,128)S(1)} %slice_bitcast_fusion.2.first_ref), channel_id=1, source_target_pairs={{0,27},{4,7},{8,3},{12,15},{16,11},{20,23},{24,19},{28,31},{32,59}... | collective-permute-start | bytes 2949128 | tf_op jit(solution)/shard_map/ppermute | solution.py:219
  19.1 1.1 slice_bitcast_fusion.1
  20.2 8.9 %step0.1.c_ref = f32[48,128,128]{2,1,0:T(8,128)} custom-call(s32[1,1,2,320]{3,2,1,0:T(2,128)} %idx_a.5, s32[1,1,2,320]{3,2,1,0:T(2,128)} %idx_b.5, s32[1,1,2,320]{3,2,1,0:T(2,128)} %idx_c.5, s32[1,1,2]{2,1,0:T(1,128)} %count.5, f32[1,1,48,128,128]{4,3,2,1,0:T(8,128)} %a_ref.1, f32[1,1,48,128,128]{4,3,2,1,0:T(8,128)} %b_ref.1, f32[1,1,48,128,128]{4,3,2,1,0:T(8,128)} %c_ref.1), custom_call_target="tpu_custom_call" | custom-call | flops 5368709120 | bytes 16777216 | tf_op jit(solution)/shard_map/step0/pallas_call | solution.py:233
  29.0 5.3 %collective-permute-done = f32[17,128,128]{2,1,0:T(8,128)} collective-permute-done((f32[17,128,128]{2,1,0:T(8,128)S(1)}, f32[17,128,128]{2,1,0:T(8,128)}, u32[]{:S(2)}, u32[]{:S(2)}) %collective-permute-start) | collective-permute-done | bytes 1114144 | tf_op jit(solution)/shard_map/ppermute | solution.py:219
  34.3 1.6 %collective-permute-start.2 = (f32[17,128,128]{2,1,0:T(8,128)}, f32[17,128,128]{2,1,0:T(8,128)}, u32[]{:S(2)}, u32[]{:S(2)}) collective-permute-start(f32[17,128,128]{2,1,0:T(8,128)} %collective-permute-done), channel_id=1, source_target_pairs={{2,7},{6,3},{10,15},{14,11},{18,23},{22,19},{26,31},{30,27},{34,39... | collective-permute-start | bytes 3342344 | tf_op jit(solution)/shard_map/ppermute | solution.py:219
  35.9 5.0 %collective-permute-start.1 = (f32[16,128,128]{2,1,0:T(8,128)}, f32[16,128,128]{2,1,0:T(8,128)}, u32[]{:S(2)}, u32[]{:S(2)}) collective-permute-start(f32[16,128,128]{2,1,0:T(8,128)} %slice_bitcast_fusion.1), channel_id=1, source_target_pairs={{0,31},{4,3},{8,7},{12,11},{16,15},{20,19},{24,23},{28,27},{32,63}... | collective-permute-start | bytes 3145736 | tf_op jit(solution)/shard_map/ppermute | solution.py:219
  40.9 0.0 collective-permute-done.5
  40.9 1.7 %collective-permute-start.6 = (f32[15,128,128]{2,1,0:T(8,128)}, f32[15,128,128]{2,1,0:T(8,128)}, u32[]{:S(2)}, u32[]{:S(2)}) collective-permute-start(f32[15,128,128]{2,1,0:T(8,128)} %collective-permute-done.5), channel_id=1, source_target_pairs={{3,7},{7,3},{11,15},{15,11},{19,23},{23,19},{27,31},{31,27},{35,39... | collective-permute-start | bytes 2949128 | tf_op jit(solution)/shard_map/ppermute | solution.py:219
  44.0 0.0 collective-permute-done.3.source
  44.0 4.5 %halves.1 = (bf16[48,128,256]{2,1,0:T(8,128)(2,1)S(1)}, s32[3,384]{1,0:T(4,128)}) custom-call(s32[1,1,2,320]{3,2,1,0:T(2,128)} %idx_a.5, s32[1,1,2,320]{3,2,1,0:T(2,128)} %idx_b.5, s32[1,1,2,320]{3,2,1,0:T(2,128)} %idx_c.5, s32[1,1,2]{2,1,0:T(1,128)} %count.5, s32[1,1]{1,0:T(1,128)S(6)} %copy.11.diag, f32[1,1,48,128,128]{4,3,2,1,0:T(8,128)} %collective-permute-done.3.source), custom_call_target="tpu_custom_call" | custom-call | flops 1048576 | bytes 6291456 | tf_op jit(solution)/shard_map/halves/pallas_call | solution.py:254
  48.5 0.0 copy-start
  48.5 1.7 %copy-done = bf16[48,128,256]{2,1,0:T(8,128)(2,1)} copy-done((bf16[48,128,256]{2,1,0:T(8,128)(2,1)}, bf16[48,128,256]{2,1,0:T(8,128)(2,1)S(1)}, u32[]{:S(2)}) %copy-start) | copy-done | bytes 3145752
  50.2 13.3 %collective-permute-done.1.last_wrap = f32[16,128,128]{2,1,0:T(8,128)} collective-permute-done((f32[16,128,128]{2,1,0:T(8,128)}, f32[16,128,128]{2,1,0:T(8,128)}, u32[]{:S(2)}, u32[]{:S(2)}) %collective-permute-start.1) | collective-permute-done | bytes 1048608 | tf_op jit(solution)/shard_map/ppermute | solution.py:219
  63.5 0.0 collective-permute-done.2.mid_wrap
  63.5 0.0 collective-permute-done.6.first_wrap
  63.5 13.1 %collective-permute-done.4.inner = f32[1,1,48,128,128]{4,3,2,1,0:T(8,128)} collective-permute-done((f32[1,1,48,128,128]{4,3,2,1,0:T(8,128)S(1)}, f32[1,1,48,128,128]{4,3,2,1,0:T(8,128)}, u32[]{:S(2)}, u32[]{:S(2)}) %collective-permute-start.4) | collective-permute-done | bytes 3145760 | tf_op jit(solution)/shard_map/ppermute | solution.py:219
  76.5 5.5 %trace_term.1 = f32[256,128]{1,0:T(8,128)} custom-call(s32[3,384]{1,0:T(4,128)} %get-tuple-element.25.listing, s32[1,1]{1,0:T(1,128)S(6)} %copy.11.diag, s32[1]{0:T(128)S(6)} %add.8.wraps, f32[1,1,48,128,128]{4,3,2,1,0:T(8,128)} %collective-permute-done.4.inner, f32[16,128,128]{2,1,0:T(8,128)} %collective-permute-done.1.last_wrap, ...), custom_call_target="tpu_custom_call" | custom-call | flops 268435456 | bytes 1048576 | tf_op jit(solution)/shard_map/trace_term/pallas_call | solution.py:267
  82.1 30.3 %all-to-all-start = ((f32[256,1,128]{2,1,0:T(1,128)}), f32[256,1,128]{2,1,0:T(1,128)S(1)}, u32[]{:S(2)}, u32[]{:S(2)}) async-start(f32[256,1,128]{2,1,0:T(1,128)} %bitcast.14), calls=%async_computation | async-start | bytes 262144 | tf_op jit(solution)/shard_map/all_to_all | solution.py:282
  112.3 12.9 %step1.1 = f32[48,128,128]{2,1,0:T(8,128)} custom-call(s32[1,1,2,320]{3,2,1,0:T(2,128)} %idx_a.5, s32[1,1,2,320]{3,2,1,0:T(2,128)} %idx_b.5, s32[1,1,2,320]{3,2,1,0:T(2,128)} %idx_c.5, s32[1,1,2]{2,1,0:T(1,128)} %count.5, s32[1]{0:T(128)S(6)} %add.8.wraps, f32[1,1,48,128,128]{4,3,2,1,0:T(8,128)} %collective-permute-done.4.inner, ...), custom_call_target="tpu_custom_call" | custom-call | flops 5368709120 | bytes 16777216 | tf_op jit(solution)/shard_map/step1/pallas_call | solution.py:283
  125.2 0.0 all-to-all-done
  125.2 0.6 slice_reduce_fusion
Async XLA Ops:
  0.6 6.7 %copy-start.1 = (f32[1,1,48,128,128]{4,3,2,1,0:T(8,128)S(1)}, f32[1,1,48,128,128]{4,3,2,1,0:T(8,128)}, u32[]{:S(2)}) copy-start(f32[1,1,48,128,128]{4,3,2,1,0:T(8,128)} %a_ref.1) | copy-start | bytes 9437188
  4.0 40.0 %collective-permute-start.3 = (f32[1,1,48,128,128]{4,3,2,1,0:T(8,128)}, f32[1,1,48,128,128]{4,3,2,1,0:T(8,128)}, u32[]{:S(2)}, u32[]{:S(2)}) collective-permute-start(f32[1,1,48,128,128]{4,3,2,1,0:T(8,128)} %b_ref.1), channel_id=1, source_target_pairs={{32,0},{64,32},{96,64},{128,96},{160,128},{192,160},{224,192},{0,2... | collective-permute-start | bytes 9437192 | tf_op jit(solution)/shard_map/ppermute | solution.py:232
  7.3 69.3 %collective-permute-start.4 = (f32[1,1,48,128,128]{4,3,2,1,0:T(8,128)S(1)}, f32[1,1,48,128,128]{4,3,2,1,0:T(8,128)}, u32[]{:S(2)}, u32[]{:S(2)}) collective-permute-start(f32[1,1,48,128,128]{4,3,2,1,0:T(8,128)S(1)} %copy-done.1), channel_id=1, source_target_pairs={{1,0},{2,1},{3,2},{5,4},{6,5},{7,6},{9,8},{10,9},{11,10},{13,12},{... | collective-permute-start | bytes 9437192 | tf_op jit(solution)/shard_map/ppermute | solution.py:219
  8.6 25.7 %collective-permute-start = (f32[17,128,128]{2,1,0:T(8,128)S(1)}, f32[17,128,128]{2,1,0:T(8,128)}, u32[]{:S(2)}, u32[]{:S(2)}) collective-permute-start(f32[17,128,128]{2,1,0:T(8,128)S(1)} %slice_bitcast_fusion.mid_ref), channel_id=1, source_target_pairs={{0,26},{4,6},{8,2},{12,14},{16,10},{20,22},{24,18},{28,30},{32,58}... | collective-permute-start | bytes 3342344 | tf_op jit(solution)/shard_map/ppermute | solution.py:219
  15.8 25.1 %collective-permute-start.5 = (f32[15,128,128]{2,1,0:T(8,128)S(1)}, f32[15,128,128]{2,1,0:T(8,128)}, u32[]{:S(2)}, u32[]{:S(2)}) collective-permute-start(f32[15,128,128]{2,1,0:T(8,128)S(1)} %slice_bitcast_fusion.2.first_ref), channel_id=1, source_target_pairs={{0,27},{4,7},{8,3},{12,15},{16,11},{20,23},{24,19},{28,31},{32,59}... | collective-permute-start | bytes 2949128 | tf_op jit(solution)/shard_map/ppermute | solution.py:219
  34.3 29.2 %collective-permute-start.2 = (f32[17,128,128]{2,1,0:T(8,128)}, f32[17,128,128]{2,1,0:T(8,128)}, u32[]{:S(2)}, u32[]{:S(2)}) collective-permute-start(f32[17,128,128]{2,1,0:T(8,128)} %collective-permute-done), channel_id=1, source_target_pairs={{2,7},{6,3},{10,15},{14,11},{18,23},{22,19},{26,31},{30,27},{34,39... | collective-permute-start | bytes 3342344 | tf_op jit(solution)/shard_map/ppermute | solution.py:219
  35.9 27.5 %collective-permute-start.1 = (f32[16,128,128]{2,1,0:T(8,128)}, f32[16,128,128]{2,1,0:T(8,128)}, u32[]{:S(2)}, u32[]{:S(2)}) collective-permute-start(f32[16,128,128]{2,1,0:T(8,128)} %slice_bitcast_fusion.1), channel_id=1, source_target_pairs={{0,31},{4,3},{8,7},{12,11},{16,15},{20,19},{24,23},{28,27},{32,63}... | collective-permute-start | bytes 3145736 | tf_op jit(solution)/shard_map/ppermute | solution.py:219
  40.9 22.6 %collective-permute-start.6 = (f32[15,128,128]{2,1,0:T(8,128)}, f32[15,128,128]{2,1,0:T(8,128)}, u32[]{:S(2)}, u32[]{:S(2)}) collective-permute-start(f32[15,128,128]{2,1,0:T(8,128)} %collective-permute-done.5), channel_id=1, source_target_pairs={{3,7},{7,3},{11,15},{15,11},{19,23},{23,19},{27,31},{31,27},{35,39... | collective-permute-start | bytes 2949128 | tf_op jit(solution)/shard_map/ppermute | solution.py:219
  48.5 1.7 %copy-start = (bf16[48,128,256]{2,1,0:T(8,128)(2,1)}, bf16[48,128,256]{2,1,0:T(8,128)(2,1)S(1)}, u32[]{:S(2)}) copy-start(bf16[48,128,256]{2,1,0:T(8,128)(2,1)S(1)} %get-tuple-element.23.right) | copy-start | bytes 9437188
  82.1 43.2 %all-to-all-start = ((f32[256,1,128]{2,1,0:T(1,128)}), f32[256,1,128]{2,1,0:T(1,128)S(1)}, u32[]{:S(2)}, u32[]{:S(2)}) async-start(f32[256,1,128]{2,1,0:T(1,128)} %bitcast.14), calls=%async_computation | async-start | bytes 262144 | tf_op jit(solution)/shard_map/all_to_all | solution.py:282

commit v3 on v2

--- a/solution.py
+++ b/solution.py
@@ -41,7 +41,7 @@
 
 
 INNER = route(lambda x, y, z, k: x >= 1, lambda x, y, z, k: (x - 1, y, z, k))
-TO_3 = route(lambda x, y, z, k: x == 0, lambda x, y, z, k: (3, y_of(y, z), z, k))
+RING = INNER + route(lambda x, y, z, k: x == 0, lambda x, y, z, k: (3, y_of(y, z), z, k))
 TO_2 = route(lambda x, y, z, k: x == 0, lambda x, y, z, k: (2, y_of(y, z), z, k))
 DIRECT = route(lambda x, y, z, k: x == 0, lambda x, y, z, k: (3, y_of(y, z), z + 4, k))
 FROM_2 = route(lambda x, y, z, k: x == 2, lambda x, y, z, k: (3, y, z + 4, k))
@@ -111,7 +111,7 @@
     load(acc.at[pl.ds(0, blocks)], out_ref, sems.at[3]).wait()
 
 
-def halve_kernel(idx_a, idx_b, idx_c, count, diag, source, target, listing, staged, sem):
+def halve_kernel(idx_a, idx_b, idx_c, count, diag, source, target, listing, staged, halved, sem):
     copy = load(source.at[0, 0], staged, sem)
 
     def collect(pair, found):
@@ -125,17 +125,19 @@
         listing[1, found + i] = 0
     listing[2, 0] = found
     copy.wait()
-    halve(staged, target, 0, staged.shape[0])
+    halve(staged, halved, 0, staged.shape[0])
+    load(halved, target, sem).wait()
 
 
 def second_kernel(
     idx_a, idx_b, idx_c, count, wraps,
-    inner, last_wrap, mid_wrap, first_wrap, right, c_ref,
-    out_ref, acc, a_in, left, sems,
+    first_in, rest_in, last_wrap, mid_wrap, first_wrap, right_in, c_ref,
+    out_ref, acc, a_in, left, right, sems,
 ):
     blocks = a_in.shape[0]
     spots = [a_in.at[pl.ds(at, size)] for at, size in zip(FIRST, PARTS)]
     wrapped = [first_wrap, mid_wrap, last_wrap]
+    straight = [first_in] + [rest_in.at[pl.ds(FIRST[i] - FIRST[1], PARTS[i])] for i in (1, 2)]
 
     @pl.when(wraps[0] == 1)
     def _():
@@ -145,47 +147,58 @@
     @pl.when(wraps[0] == 0)
     def _():
         for i in range(3):
-            load(inner.at[0, 0, pl.ds(FIRST[i], PARTS[i])], spots[i], sems.at[i])
-
+            load(straight[i], spots[i], sems.at[i])
+
+    b_copy = load(right_in, right, sems.at[3])
     c_copy = load(c_ref, acc.at[pl.ds(0, blocks)], sems.at[4])
     for i in range(3):
         pltpu.make_async_copy(wrapped[i], spots[i], sems.at[i]).wait()
         halve(a_in, left, FIRST[i], PARTS[i])
+    b_copy.wait()
     c_copy.wait()
     multiply(1, idx_a, idx_b, idx_c, count, left, right, acc)
-    load(acc.at[pl.ds(0, blocks)], out_ref, sems.at[3]).wait()
+    load(acc.at[pl.ds(0, blocks)], out_ref, sems.at[5]).wait()
 
 
 def trace_kernel(
-    listing, diag, wraps, inner, last_wrap, mid_wrap, first_wrap, right, c_ref, term_ref, a_in, total, sem, c_sem
+    listing, diag, wraps, first_in, rest_in, last_wrap, mid_wrap, first_wrap, right, c_ref,
+    term_ref, a_in, b_in, total, a_sem, b_sem, c_sem,
 ):
     found = listing[2, 0]
-    load(c_ref.at[diag[0, 0]], total, c_sem).wait()
-    parts = [first_wrap, mid_wrap, last_wrap]
+    c_copy = load(c_ref.at[diag[0, 0]], total, c_sem)
+    wrapped = [first_wrap, mid_wrap, last_wrap]
+    wraps_here = wraps[0] == 1
 
     def batch(g, carry):
         for i in range(BATCH):
+            load(right.at[listing[1, g * BATCH + i]], b_in.at[i], b_sem)
             block = listing[0, g * BATCH + i]
             part = (block >= FIRST[1]).astype(jnp.int32) + (block >= FIRST[2]).astype(jnp.int32)
 
-            @pl.when(wraps[0] == 0)
+            @pl.when(jnp.logical_and(jnp.logical_not(wraps_here), part == 0))
             def _():
-                load(inner.at[0, 0, block], a_in.at[i], sem)
+                load(first_in.at[block], a_in.at[i], a_sem)
+
+            @pl.when(jnp.logical_and(jnp.logical_not(wraps_here), part > 0))
+            def _():
+                load(rest_in.at[block - FIRST[1]], a_in.at[i], a_sem)
 
             for j in range(3):
 
-                @pl.when(jnp.logical_and(wraps[0] == 1, part == j))
+                @pl.when(jnp.logical_and(wraps_here, part == j))
                 def _():
-                    load(parts[j].at[block - FIRST[j]], a_in.at[i], sem)
-
-        pltpu.make_async_copy(inner.at[0, 0, pl.ds(0, BATCH)], a_in, sem).wait()
+                    load(wrapped[j].at[block - FIRST[j]], a_in.at[i], a_sem)
+
+        pltpu.make_async_copy(right.at[pl.ds(0, BATCH)], b_in, b_sem).wait()
+        pltpu.make_async_copy(rest_in.at[pl.ds(0, BATCH)], a_in, a_sem).wait()
         for i in range(BATCH):
-            halves_of = jnp.concatenate(split(a_in[i]), axis=1)
-            weights = right[listing[1, g * BATCH + i]]
-            both = jnp.dot(halves_of, jnp.concatenate([weights, weights], axis=0), preferred_element_type=jnp.float32)
+            halves = jnp.concatenate(split(a_in[i]), axis=1)
+            weights = b_in[i]
+            both = jnp.dot(halves, jnp.concatenate([weights, weights], axis=0), preferred_element_type=jnp.float32)
             total[...] += jnp.where(g * BATCH + i < found, both[:, :BS] + both[:, BS:], 0.0)
         return carry
 
+    c_copy.wait()
     lax.fori_loop(0, lax.div(found + BATCH - 1, BATCH), batch, 0)
     eye = lax.broadcasted_iota(jnp.int32, (BS, BS), 0) == lax.broadcasted_iota(jnp.int32, (BS, BS), 1)
     picked = jnp.where(eye, total[...], 0.0)
@@ -195,22 +208,6 @@
 SMEM = pl.BlockSpec(memory_space=pltpu.SMEM)
 VMEM = pl.BlockSpec(memory_space=pltpu.VMEM)
 HBM = pl.BlockSpec(memory_space=pl.ANY)
-
-
-def behind_kernel(first_ref, mid_ref, token_ref):
-    token_ref[0, 0] = 0
-
-
-def behind(*arrays):
-    return pl.pallas_call(
-        behind_kernel,
-        in_specs=[HBM] * len(arrays),
-        out_specs=SMEM,
-        out_shape=jax.ShapeDtypeStruct((1, 1), jnp.int32),
-        compiler_params=pltpu.CompilerParams(vmem_limit_bytes=24 * MIB),
-        cost_estimate=pl.CostEstimate(flops=0, bytes_accessed=4 * MIB, transcendentals=0),
-        name="behind",
-    )(*arrays)
 
 
 def local(a_blocks, b_blocks, c_prior, pair_a, pair_b, pair_c, pair_count, diag_slot):
@@ -224,12 +221,9 @@
     cost = pl.CostEstimate(flops=8 * 320 * BS**3, bytes_accessed=16 * MIB, transcendentals=0)
     params = pltpu.CompilerParams(vmem_limit_bytes=56 * MIB)
 
-    a_first, a_mid = a[: FIRST[1]], a[FIRST[1] : FIRST[2]]
-    first_relay = hop(a_first, TO_3)
-    mid_relay = hop(a_mid, TO_2)
-    a_inner, b_sent, token = lax.optimization_barrier((a_blocks, b_blocks, behind(a_first, a_mid)))
-    inner = hop(a_inner, INNER)
-    b_next = lax.ppermute(b_sent, "row", ROWS)
+    first = hop(a[: FIRST[1]], RING)
+    mid_relay = hop(a[FIRST[1] : FIRST[2]], TO_2)
+    b_next = lax.ppermute(b_blocks, "row", ROWS)
     c_now = pl.pallas_call(
         first_kernel,
         in_specs=[SMEM] * 4 + [HBM] * 3,
@@ -247,54 +241,63 @@
         cost_estimate=cost,
         name="step0",
     )(*lists, a_blocks, b_blocks, c_prior)
-    a_last, mid_relay, c_now = lax.optimization_barrier((a_inner[0, 0, FIRST[2] :], mid_relay, c_now))
+    a_last, mid_relay, c_now = lax.optimization_barrier((a[FIRST[2] :], mid_relay, c_now))
     last_wrap = hop(a_last, DIRECT)
     mid_wrap = hop(mid_relay, FROM_2)
-    first_wrap = hop(first_relay, FROM_3)
+    first, a_rest, c_now = lax.optimization_barrier((first, a[FIRST[1] :], c_now))
+    first_wrap = hop(first, FROM_3)
+    rest = hop(a_rest, INNER)
     right, listing = pl.pallas_call(
         halve_kernel,
         in_specs=[SMEM] * 5 + [HBM],
-        out_specs=[VMEM, SMEM],
-        out_shape=[pltpu.VMEM(wide, jnp.bfloat16), jax.ShapeDtypeStruct((3, 384), jnp.int32)],
-        scratch_shapes=[pltpu.VMEM(whole, jnp.float32), pltpu.SemaphoreType.DMA],
+        out_specs=[HBM, SMEM],
+        out_shape=[jax.ShapeDtypeStruct(wide, jnp.bfloat16), jax.ShapeDtypeStruct((3, 384), jnp.int32)],
+        scratch_shapes=[
+            pltpu.VMEM(whole, jnp.float32),
+            pltpu.VMEM(wide, jnp.bfloat16),
+            pltpu.SemaphoreType.DMA,
+        ],
         compiler_params=params,
         cost_estimate=pl.CostEstimate(flops=MIB, bytes_accessed=6 * MIB, transcendentals=0),
         name="halves",
     )(*lists, diag_slot, b_next)
 
     wraps = (lax.axis_index("col") % 4 == 3).astype(jnp.int32)[None]
-    wraps, last_wrap, mid_wrap, right = lax.optimization_barrier((wraps + token[0, :1], last_wrap, mid_wrap, right))
+    wraps, last_wrap, mid_wrap, right = lax.optimization_barrier((wraps, last_wrap, mid_wrap, right))
     term = pl.pallas_call(
         trace_kernel,
-        in_specs=[SMEM] * 3 + [HBM] * 4 + [VMEM, HBM],
+        in_specs=[SMEM] * 3 + [HBM] * 7,
         out_specs=VMEM,
         out_shape=jax.ShapeDtypeStruct((devices, BS), jnp.float32),
         scratch_shapes=[
             pltpu.VMEM((BATCH, BS, BS), jnp.float32),
+            pltpu.VMEM((BATCH, BS, 2 * BS), jnp.bfloat16),
             pltpu.VMEM((BS, BS), jnp.float32),
+            pltpu.SemaphoreType.DMA,
             pltpu.SemaphoreType.DMA,
             pltpu.SemaphoreType.DMA,
         ],
         compiler_params=params,
         cost_estimate=pl.CostEstimate(flops=8 * BATCH * BS**3, bytes_accessed=MIB, transcendentals=0),
         name="trace_term",
-    )(listing, diag_slot, wraps, inner, last_wrap, mid_wrap, first_wrap, right, c_now)
+    )(listing, diag_slot, wraps, first, rest, last_wrap, mid_wrap, first_wrap, right, c_now)
     terms = lax.all_to_all(term, AXES, 0, 0, tiled=True)
     c_now = pl.pallas_call(
         second_kernel,
-        in_specs=[SMEM] * 5 + [HBM] * 4 + [VMEM, HBM],
+        in_specs=[SMEM] * 5 + [HBM] * 7,
         out_specs=HBM,
         out_shape=jax.ShapeDtypeStruct(whole, jnp.float32),
         scratch_shapes=[
             pltpu.VMEM(padded, jnp.float32),
             pltpu.VMEM(whole, jnp.float32),
             pltpu.VMEM(wide, jnp.bfloat16),
-            pltpu.SemaphoreType.DMA((5,)),
+            pltpu.VMEM(wide, jnp.bfloat16),
+            pltpu.SemaphoreType.DMA((6,)),
         ],
         compiler_params=params,
         cost_estimate=cost,
         name="step1",
-    )(*lists, wraps, inner, last_wrap, mid_wrap, first_wrap, right, c_now)
+    )(*lists, wraps, first, rest, last_wrap, mid_wrap, first_wrap, right, c_now)
     trace_value = jnp.sum(terms[:, 0]) / (BS * jnp.sqrt(jnp.float32(devices)))
     return (c_now[None, None], trace_value)
 

time: 128 us -> 131 us (1.023)
  waiting for transfers between devices: 31.6 us -> 26 us
  starting transfers between devices: 53.7 us -> 58.8 us
  local copies, waits for them, and re-layouts: 5.55 us -> 7.99 us
    ppermute x6, waiting for transfers between devices: 31.6 us -> 23.2 us  [local(): hop = lambda array, pairs: lax.ppermute(array, AXES, pairs)]
    ppermute x6, starting transfers between devices: 20.1 us -> 28.3 us  [local(): hop = lambda array, pairs: lax.ppermute(array, AXES, pairs)]
    pallas_call x1, Pallas kernels: 8.87 us -> 12.7 us  [local(): pl.pallas_call(first_kernel, in_specs=[SMEM] * 4 + [HBM] * 3, out_specs=H...]
    slice x2 -> x4, local copies, waits for them, and re-layouts: 2.78 us -> 6.32 us  [the longest x1 2.23 us: local(): first = hop(a[:FIRST[1]], RING)]
    all_to_all x1, waiting for transfers between devices: 0.01 us -> 2.73 us  [local(): terms = lax.all_to_all(term, AXES, 0, 0, tiled=True)]
    pallas_call x4 -> x3, Pallas kernels: 23.4 us -> 20.7 us  [the longest x1 10.1 us: local(): pl.pallas_call(second_kernel, in_specs=[SMEM] * 5 + [HBM] * 7, out_specs=...]
    ppermute x1, starting transfers between devices: 3.32 us -> 0.96 us  [local(): b_next = lax.ppermute(b_blocks, 'row', ROWS)]
  transfers between devices with their start and end apart: 8 -> 8, of which waited for: 3 -> 5; matrix products, arithmetic and copies ran while one was open for 1% -> 4% of each run, Pallas kernels for 21% -> 22%
where the time goes in v3:
time: 131 us; the launch traced here: 130 us
  starting transfers between devices  58.8 us (45%)
  Pallas kernels  33.4 us (25%)
  waiting for transfers between devices  26 us (20%)
  local copies, waits for them, and re-layouts  7.99 us (6%)
  between operations  3.15 us (2%)
    all_to_all x1, starting transfers between devices, local(): terms = lax.all_to_all(term, AXES, 0, 0, tiled=True)  29.5 us
    ppermute x6, starting transfers between devices, local(): hop = lambda array, pairs: lax.ppermute(array, AXES, pairs)  28.3 us
    ppermute x6, waiting for transfers between devices, local(): hop = lambda array, pairs: lax.ppermute(array, AXES, pairs)  23.2 us
    pallas_call x1, Pallas kernels, local(): pl.pallas_call(first_kernel, in_specs=[SMEM] * 4 + [HBM] * 3, out_specs=H...  12.7 us
    pallas_call x1, Pallas kernels, local(): pl.pallas_call(second_kernel, in_specs=[SMEM] * 5 + [HBM] * 7, out_specs=...  10.1 us
    pallas_call x1, Pallas kernels, local(): pl.pallas_call(halve_kernel, in_specs=[SMEM] * 5 + [HBM], out_specs=[HBM,...  5.55 us
    pallas_call x1, Pallas kernels, local(): pl.pallas_call(trace_kernel, in_specs=[SMEM] * 3 + [HBM] * 7, out_specs=V...  5 us
    all_to_all x1, waiting for transfers between devices, local(): terms = lax.all_to_all(term, AXES, 0, 0, tiled=True)  2.73 us
  transfers between devices with their start and end apart: 8, of which 5 were waited for; matrix products, arithmetic and copies ran while one was open for 4% of the time, Pallas kernels for 22%

profile of v3, /device:TPU:1, one launch (start us, length us, event | category | flops | bytes accessed | tf_op | source)
XLA Modules:
  0.0 129.9 jit_solution(13865585439716204829)
XLA Ops:
  0.6 0.0 copy-start
  0.6 1.5 %slice_bitcast_fusion.1 = f32[17,128,128]{2,1,0:T(8,128)S(1)} fusion(f32[1,1,48,128,128]{4,3,2,1,0:T(8,128)} %a_ref.1), kind=kLoop, calls=%fused_computation.1 | loop fusion | bytes 2228224 | tf_op jit(solution)/shard_map/slice | solution.py:225
  2.1 9.0 %collective-permute-start = (f32[17,128,128]{2,1,0:T(8,128)S(1)}, f32[17,128,128]{2,1,0:T(8,128)}, u32[]{:S(2)}, u32[]{:S(2)}) collective-permute-start(f32[17,128,128]{2,1,0:T(8,128)S(1)} %slice_bitcast_fusion.1), channel_id=1, source_target_pairs={{0,26},{4,6},{8,2},{12,14},{16,10},{20,22},{24,18},{28,30},{32,58}... | collective-permute-start | bytes 3342344 | tf_op jit(solution)/shard_map/ppermute | solution.py:216
  11.1 1.0 collective-permute-start.3
  12.1 2.2 %slice_bitcast_fusion.3 = f32[15,128,128]{2,1,0:T(8,128)} fusion(f32[1,1,48,128,128]{4,3,2,1,0:T(8,128)} %a_ref.1), kind=kLoop, calls=%fused_computation.3 | loop fusion | bytes 1966080 | tf_op jit(solution)/shard_map/slice | solution.py:224
  14.3 0.0 collective-permute-start.4
  14.3 0.0 copy-done
  14.3 1.1 slice_bitcast_fusion.2
  15.4 1.5 %slice_bitcast_fusion = f32[33,128,128]{2,1,0:T(8,128)} fusion(f32[1,1,48,128,128]{4,3,2,1,0:T(8,128)S(1)} %copy-done), kind=kLoop, calls=%fused_computation | loop fusion | bytes 4325376 | tf_op jit(solution)/shard_map/slice | solution.py:247
  16.9 12.7 %step0.1.c_ref = f32[48,128,128]{2,1,0:T(8,128)} custom-call(s32[1,1,2,320]{3,2,1,0:T(2,128)} %idx_a.5, s32[1,1,2,320]{3,2,1,0:T(2,128)} %idx_b.5, s32[1,1,2,320]{3,2,1,0:T(2,128)} %idx_c.5, s32[1,1,2]{2,1,0:T(1,128)} %count.5, f32[1,1,48,128,128]{4,3,2,1,0:T(8,128)} %a_ref.1, f32[1,1,48,128,128]{4,3,2,1,0:T(8,128)} %b_ref.1, f32[1,1,48,128,128]{4,3,2,1,0:T(8,128)} %c_ref.1), custom_call_target="tpu_custom_call" | custom-call | flops 5368709120 | bytes 16777216 | tf_op jit(solution)/shard_map/step0/pallas_call | solution.py:227
  29.6 3.7 %collective-permute-done = f32[17,128,128]{2,1,0:T(8,128)} collective-permute-done((f32[17,128,128]{2,1,0:T(8,128)S(1)}, f32[17,128,128]{2,1,0:T(8,128)}, u32[]{:S(2)}, u32[]{:S(2)}) %collective-permute-start) | collective-permute-done | bytes 1114144 | tf_op jit(solution)/shard_map/ppermute | solution.py:216
  33.3 0.8 collective-permute-done.4.first_in
  34.1 1.3 collective-permute-start.5
  35.4 1.7 %collective-permute-start.2 = (f32[17,128,128]{2,1,0:T(8,128)}, f32[17,128,128]{2,1,0:T(8,128)}, u32[]{:S(2)}, u32[]{:S(2)}) collective-permute-start(f32[17,128,128]{2,1,0:T(8,128)} %collective-permute-done), channel_id=1, source_target_pairs={{2,7},{6,3},{10,15},{14,11},{18,23},{22,19},{26,31},{30,27},{34,39... | collective-permute-start | bytes 3342344 | tf_op jit(solution)/shard_map/ppermute | solution.py:216
  37.0 14.8 %collective-permute-start.1 = (f32[16,128,128]{2,1,0:T(8,128)}, f32[16,128,128]{2,1,0:T(8,128)}, u32[]{:S(2)}, u32[]{:S(2)}) collective-permute-start(f32[16,128,128]{2,1,0:T(8,128)} %slice_bitcast_fusion.2), channel_id=1, source_target_pairs={{0,31},{4,3},{8,7},{12,11},{16,15},{20,19},{24,23},{28,27},{32,63}... | collective-permute-start | bytes 3145736 | tf_op jit(solution)/shard_map/ppermute | solution.py:216
  51.8 1.6 %collective-permute-start.6 = (f32[15,128,128]{2,1,0:T(8,128)}, f32[15,128,128]{2,1,0:T(8,128)}, u32[]{:S(2)}, u32[]{:S(2)}) collective-permute-start(f32[15,128,128]{2,1,0:T(8,128)} %collective-permute-done.4.first_in), channel_id=1, source_target_pairs={{3,7},{7,3},{11,15},{15,11},{19,23},{23,19},{27,31},{31,27},{35,39... | collective-permute-start | bytes 2949128 | tf_op jit(solution)/shard_map/ppermute | solution.py:216
  54.1 0.0 collective-permute-done.3.source
  54.1 0.0 copy-start.1
  54.1 1.7 %copy-done.1 = f32[1,1,48,128,128]{4,3,2,1,0:T(8,128)} copy-done((f32[1,1,48,128,128]{4,3,2,1,0:T(8,128)}, f32[1,1,48,128,128]{4,3,2,1,0:T(8,128)S(1)}, u32[]{:S(2)}) %copy-start.1) | copy-done | bytes 3145752
  55.8 5.6 %halves.1 = (bf16[48,128,256]{2,1,0:T(8,128)(2,1)}, s32[3,384]{1,0:T(4,128)}) custom-call(s32[1,1,2,320]{3,2,1,0:T(2,128)} %idx_a.5, s32[1,1,2,320]{3,2,1,0:T(2,128)} %idx_b.5, s32[1,1,2,320]{3,2,1,0:T(2,128)} %idx_c.5, s32[1,1,2]{2,1,0:T(1,128)} %count.5, s32[1,1]{1,0:T(1,128)S(6)} %copy.11.diag, f32[1,1,48,128,128]{4,3,2,1,0:T(8,128)} %copy-done.1), custom_call_target="tpu_custom_call" | custom-call | flops 1048576 | bytes 6291456 | tf_op jit(solution)/shard_map/halves/pallas_call | solution.py:250
  61.3 10.5 %collective-permute-done.1.last_wrap = f32[16,128,128]{2,1,0:T(8,128)} collective-permute-done((f32[16,128,128]{2,1,0:T(8,128)}, f32[16,128,128]{2,1,0:T(8,128)}, u32[]{:S(2)}, u32[]{:S(2)}) %collective-permute-start.1) | collective-permute-done | bytes 1048608 | tf_op jit(solution)/shard_map/ppermute | solution.py:216
  71.9 0.0 collective-permute-done.2.mid_wrap
  71.9 0.0 collective-permute-done.6.first_wrap
  71.9 8.2 %collective-permute-done.5.rest_in = f32[33,128,128]{2,1,0:T(8,128)} collective-permute-done((f32[33,128,128]{2,1,0:T(8,128)}, f32[33,128,128]{2,1,0:T(8,128)}, u32[]{:S(2)}, u32[]{:S(2)}) %collective-permute-start.5) | collective-permute-done | bytes 2162720 | tf_op jit(solution)/shard_map/ppermute | solution.py:216
  80.1 5.0 %trace_term.1 = f32[256,128]{1,0:T(8,128)} custom-call(s32[3,384]{1,0:T(4,128)} %get-tuple-element.25.listing, s32[1,1]{1,0:T(1,128)S(6)} %copy.11.diag, s32[1]{0:T(128)} %bitcast.wraps, f32[15,128,128]{2,1,0:T(8,128)} %collective-permute-done.4.first_in, f32[33,128,128]{2,1,0:T(8,128)} %collective-permute-done.5.rest_in, ...), custom_call_target="tpu_custom_call" | custom-call | flops 268435456 | bytes 1048576 | tf_op jit(solution)/shard_map/trace_term/pallas_call | solution.py:267
  85.1 29.5 %all-to-all-start = ((f32[256,1,128]{2,1,0:T(1,128)}), f32[256,1,128]{2,1,0:T(1,128)S(1)}, u32[]{:S(2)}, u32[]{:S(2)}) async-start(f32[256,1,128]{2,1,0:T(1,128)} %bitcast.15), calls=%async_computation | async-start | bytes 262144 | tf_op jit(solution)/shard_map/all_to_all | solution.py:284
  114.6 10.1 %step1.1 = f32[48,128,128]{2,1,0:T(8,128)} custom-call(s32[1,1,2,320]{3,2,1,0:T(2,128)} %idx_a.5, s32[1,1,2,320]{3,2,1,0:T(2,128)} %idx_b.5, s32[1,1,2,320]{3,2,1,0:T(2,128)} %idx_c.5, s32[1,1,2]{2,1,0:T(1,128)} %count.5, s32[1]{0:T(128)} %bitcast.wraps, f32[15,128,128]{2,1,0:T(8,128)} %collective-permute-done.4.first_in, ...), custom_call_target="tpu_custom_call" | custom-call | flops 5368709120 | bytes 16777216 | tf_op jit(solution)/shard_map/step1/pallas_call | solution.py:285
  124.7 2.7 %all-to-all-done = f32[256,1,128]{2,1,0:T(1,128)S(1)} async-done(((f32[256,1,128]{2,1,0:T(1,128)}), f32[256,1,128]{2,1,0:T(1,128)S(1)}, u32[]{:S(2)}, u32[]{:S(2)}) %all-to-all-start) | async-done | bytes 131104 | tf_op jit(solution)/shard_map/all_to_all | solution.py:284
  127.5 0.6 slice_reduce_fusion
Async XLA Ops:
  0.6 13.7 %copy-start = (f32[1,1,48,128,128]{4,3,2,1,0:T(8,128)S(1)}, f32[1,1,48,128,128]{4,3,2,1,0:T(8,128)}, u32[]{:S(2)}) copy-start(f32[1,1,48,128,128]{4,3,2,1,0:T(8,128)} %a_ref.1) | copy-start | bytes 9437188
  2.1 31.1 %collective-permute-start = (f32[17,128,128]{2,1,0:T(8,128)S(1)}, f32[17,128,128]{2,1,0:T(8,128)}, u32[]{:S(2)}, u32[]{:S(2)}) collective-permute-start(f32[17,128,128]{2,1,0:T(8,128)S(1)} %slice_bitcast_fusion.1), channel_id=1, source_target_pairs={{0,26},{4,6},{8,2},{12,14},{16,10},{20,22},{24,18},{28,30},{32,58}... | collective-permute-start | bytes 3342344 | tf_op jit(solution)/shard_map/ppermute | solution.py:216
  11.1 43.0 %collective-permute-start.3 = (f32[1,1,48,128,128]{4,3,2,1,0:T(8,128)}, f32[1,1,48,128,128]{4,3,2,1,0:T(8,128)S(1)}, u32[]{:S(2)}, u32[]{:S(2)}) collective-permute-start(f32[1,1,48,128,128]{4,3,2,1,0:T(8,128)} %b_ref.1), channel_id=1, source_target_pairs={{32,0},{64,32},{96,64},{128,96},{160,128},{192,160},{224,192},{0,2... | collective-permute-start | bytes 9437192 | tf_op jit(solution)/shard_map/ppermute | solution.py:226
  14.3 19.8 %collective-permute-start.4 = (f32[15,128,128]{2,1,0:T(8,128)}, f32[15,128,128]{2,1,0:T(8,128)}, u32[]{:S(2)}, u32[]{:S(2)}) collective-permute-start(f32[15,128,128]{2,1,0:T(8,128)} %slice_bitcast_fusion.3), channel_id=1, source_target_pairs={{1,0},{2,1},{3,2},{5,4},{6,5},{7,6},{9,8},{10,9},{11,10},{13,12},{... | collective-permute-start | bytes 2949128 | tf_op jit(solution)/shard_map/ppermute | solution.py:216
  34.1 46.0 %collective-permute-start.5 = (f32[33,128,128]{2,1,0:T(8,128)}, f32[33,128,128]{2,1,0:T(8,128)}, u32[]{:S(2)}, u32[]{:S(2)}) collective-permute-start(f32[33,128,128]{2,1,0:T(8,128)} %slice_bitcast_fusion), channel_id=1, source_target_pairs={{1,0},{2,1},{3,2},{5,4},{6,5},{7,6},{9,8},{10,9},{11,10},{13,12},{... | collective-permute-start | bytes 6488072 | tf_op jit(solution)/shard_map/ppermute | solution.py:216
  35.4 36.5 %collective-permute-start.2 = (f32[17,128,128]{2,1,0:T(8,128)}, f32[17,128,128]{2,1,0:T(8,128)}, u32[]{:S(2)}, u32[]{:S(2)}) collective-permute-start(f32[17,128,128]{2,1,0:T(8,128)} %collective-permute-done), channel_id=1, source_target_pairs={{2,7},{6,3},{10,15},{14,11},{18,23},{22,19},{26,31},{30,27},{34,39... | collective-permute-start | bytes 3342344 | tf_op jit(solution)/shard_map/ppermute | solution.py:216
  37.0 34.8 %collective-permute-start.1 = (f32[16,128,128]{2,1,0:T(8,128)}, f32[16,128,128]{2,1,0:T(8,128)}, u32[]{:S(2)}, u32[]{:S(2)}) collective-permute-start(f32[16,128,128]{2,1,0:T(8,128)} %slice_bitcast_fusion.2), channel_id=1, source_target_pairs={{0,31},{4,3},{8,7},{12,11},{16,15},{20,19},{24,23},{28,27},{32,63}... | collective-permute-start | bytes 3145736 | tf_op jit(solution)/shard_map/ppermute | solution.py:216
  51.8 20.1 %collective-permute-start.6 = (f32[15,128,128]{2,1,0:T(8,128)}, f32[15,128,128]{2,1,0:T(8,128)}, u32[]{:S(2)}, u32[]{:S(2)}) collective-permute-start(f32[15,128,128]{2,1,0:T(8,128)} %collective-permute-done.4.first_in), channel_id=1, source_target_pairs={{3,7},{7,3},{11,15},{15,11},{19,23},{23,19},{27,31},{31,27},{35,39... | collective-permute-start | bytes 2949128 | tf_op jit(solution)/shard_map/ppermute | solution.py:216
  54.1 1.7 %copy-start.1 = (f32[1,1,48,128,128]{4,3,2,1,0:T(8,128)}, f32[1,1,48,128,128]{4,3,2,1,0:T(8,128)S(1)}, u32[]{:S(2)}) copy-start(f32[1,1,48,128,128]{4,3,2,1,0:T(8,128)S(1)} %collective-permute-done.3.source) | copy-start | bytes 9437188
  85.1 42.4 %all-to-all-start = ((f32[256,1,128]{2,1,0:T(1,128)}), f32[256,1,128]{2,1,0:T(1,128)S(1)}, u32[]{:S(2)}, u32[]{:S(2)}) async-start(f32[256,1,128]{2,1,0:T(1,128)} %bitcast.15), calls=%async_computation | async-start | bytes 262144 | tf_op jit(solution)/shard_map/all_to_all | solution.py:284

commit v4 on v3

--- a/solution.py
+++ b/solution.py
@@ -9,7 +9,7 @@
 BS = 128
 UNROLL = 64
 BATCH = 16
-PARTS = (15, 17, 16)
+PARTS = (16, 16, 16)
 FIRST = (0, PARTS[0], PARTS[0] + PARTS[1])
 MIB = 2**20
 
@@ -41,7 +41,7 @@
 
 
 INNER = route(lambda x, y, z, k: x >= 1, lambda x, y, z, k: (x - 1, y, z, k))
-RING = INNER + route(lambda x, y, z, k: x == 0, lambda x, y, z, k: (3, y_of(y, z), z, k))
+TO_3 = route(lambda x, y, z, k: x == 0, lambda x, y, z, k: (3, y_of(y, z), z, k))
 TO_2 = route(lambda x, y, z, k: x == 0, lambda x, y, z, k: (2, y_of(y, z), z, k))
 DIRECT = route(lambda x, y, z, k: x == 0, lambda x, y, z, k: (3, y_of(y, z), z + 4, k))
 FROM_2 = route(lambda x, y, z, k: x == 2, lambda x, y, z, k: (3, y, z + 4, k))
@@ -111,7 +111,9 @@
     load(acc.at[pl.ds(0, blocks)], out_ref, sems.at[3]).wait()
 
 
-def halve_kernel(idx_a, idx_b, idx_c, count, diag, source, target, listing, staged, halved, sem):
+def halve_kernel(
+    idx_a, idx_b, idx_c, count, diag, source, target, picked, listing, staged, halved, sem
+):
     copy = load(source.at[0, 0], staged, sem)
 
     def collect(pair, found):
@@ -126,18 +128,21 @@
     listing[2, 0] = found
     copy.wait()
     halve(staged, halved, 0, staged.shape[0])
-    load(halved, target, sem).wait()
+    out = load(halved, target, sem)
+    for i in range(BATCH):
+        picked[i] = halved[listing[1, i]]
+    out.wait()
 
 
 def second_kernel(
     idx_a, idx_b, idx_c, count, wraps,
-    first_in, rest_in, last_wrap, mid_wrap, first_wrap, right_in, c_ref,
+    inner, last_wrap, mid_wrap, first_wrap, right_in, c_ref,
     out_ref, acc, a_in, left, right, sems,
 ):
     blocks = a_in.shape[0]
     spots = [a_in.at[pl.ds(at, size)] for at, size in zip(FIRST, PARTS)]
     wrapped = [first_wrap, mid_wrap, last_wrap]
-    straight = [first_in] + [rest_in.at[pl.ds(FIRST[i] - FIRST[1], PARTS[i])] for i in (1, 2)]
+    straight = [inner.at[0, 0, pl.ds(at, size)] for at, size in zip(FIRST, PARTS)]
 
     @pl.when(wraps[0] == 1)
     def _():
@@ -161,36 +166,43 @@
 
 
 def trace_kernel(
-    listing, diag, wraps, first_in, rest_in, last_wrap, mid_wrap, first_wrap, right, c_ref,
-    term_ref, a_in, b_in, total, a_sem, b_sem, c_sem,
+    listing, diag, wraps, inner, last_wrap, mid_wrap, first_wrap, right, picked, c_ref,
+    term_ref, a_in, b_in, c_in, total, a_sem, b_sem, c_sem,
 ):
     found = listing[2, 0]
-    c_copy = load(c_ref.at[diag[0, 0]], total, c_sem)
+    c_copy = load(c_ref.at[diag[0, 0]], c_in, c_sem)
     wrapped = [first_wrap, mid_wrap, last_wrap]
     wraps_here = wraps[0] == 1
+    total[...] = jnp.zeros_like(total)
 
     def batch(g, carry):
-        for i in range(BATCH):
-            load(right.at[listing[1, g * BATCH + i]], b_in.at[i], b_sem)
-            block = listing[0, g * BATCH + i]
-            part = (block >= FIRST[1]).astype(jnp.int32) + (block >= FIRST[2]).astype(jnp.int32)
-
-            @pl.when(jnp.logical_and(jnp.logical_not(wraps_here), part == 0))
-            def _():
-                load(first_in.at[block], a_in.at[i], a_sem)
-
-            @pl.when(jnp.logical_and(jnp.logical_not(wraps_here), part > 0))
-            def _():
-                load(rest_in.at[block - FIRST[1]], a_in.at[i], a_sem)
-
-            for j in range(3):
-
-                @pl.when(jnp.logical_and(wraps_here, part == j))
-                def _():
-                    load(wrapped[j].at[block - FIRST[j]], a_in.at[i], a_sem)
-
-        pltpu.make_async_copy(right.at[pl.ds(0, BATCH)], b_in, b_sem).wait()
-        pltpu.make_async_copy(rest_in.at[pl.ds(0, BATCH)], a_in, a_sem).wait()
+        @pl.when(g == 0)
+        def _():
+            load(picked, b_in, b_sem)
+
+        @pl.when(g > 0)
+        def _():
+            for i in range(BATCH):
+                load(right.at[listing[1, g * BATCH + i]], b_in.at[i], b_sem)
+
+        @pl.when(jnp.logical_not(wraps_here))
+        def _():
+            for i in range(BATCH):
+                load(inner.at[0, 0, listing[0, g * BATCH + i]], a_in.at[i], a_sem)
+
+        @pl.when(wraps_here)
+        def _():
+            for i in range(BATCH):
+                block = listing[0, g * BATCH + i]
+                part = (block >= FIRST[1]).astype(jnp.int32) + (block >= FIRST[2]).astype(jnp.int32)
+                for j in range(3):
+
+                    @pl.when(part == j)
+                    def _():
+                        load(wrapped[j].at[block - FIRST[j]], a_in.at[i], a_sem)
+
+        pltpu.make_async_copy(picked, b_in, b_sem).wait()
+        pltpu.make_async_copy(inner.at[0, 0, pl.ds(0, BATCH)], a_in, a_sem).wait()
         for i in range(BATCH):
             halves = jnp.concatenate(split(a_in[i]), axis=1)
             weights = b_in[i]
@@ -198,11 +210,11 @@
             total[...] += jnp.where(g * BATCH + i < found, both[:, :BS] + both[:, BS:], 0.0)
         return carry
 
-    c_copy.wait()
     lax.fori_loop(0, lax.div(found + BATCH - 1, BATCH), batch, 0)
     eye = lax.broadcasted_iota(jnp.int32, (BS, BS), 0) == lax.broadcasted_iota(jnp.int32, (BS, BS), 1)
-    picked = jnp.where(eye, total[...], 0.0)
-    term_ref[...] = jnp.broadcast_to(jnp.sum(picked, keepdims=True), term_ref.shape)
+    c_copy.wait()
+    picked_out = jnp.where(eye, total[...] + c_in[...], 0.0)
+    term_ref[...] = jnp.broadcast_to(jnp.sum(picked_out, keepdims=True), term_ref.shape)
 
 
 SMEM = pl.BlockSpec(memory_space=pltpu.SMEM)
@@ -221,9 +233,12 @@
     cost = pl.CostEstimate(flops=8 * 320 * BS**3, bytes_accessed=16 * MIB, transcendentals=0)
     params = pltpu.CompilerParams(vmem_limit_bytes=56 * MIB)
 
-    first = hop(a[: FIRST[1]], RING)
-    mid_relay = hop(a[FIRST[1] : FIRST[2]], TO_2)
-    b_next = lax.ppermute(b_blocks, "row", ROWS)
+    a_first, a_mid = a[: FIRST[1]], a[FIRST[1] : FIRST[2]]
+    a_first, a_mid, a_inner, b_sent = lax.optimization_barrier((a_first, a_mid, a_blocks, b_blocks))
+    first_relay = hop(a_first, TO_3)
+    mid_relay = hop(a_mid, TO_2)
+    inner = hop(a_inner, INNER)
+    b_next = lax.ppermute(b_sent, "row", ROWS)
     c_now = pl.pallas_call(
         first_kernel,
         in_specs=[SMEM] * 4 + [HBM] * 3,
@@ -241,17 +256,19 @@
         cost_estimate=cost,
         name="step0",
     )(*lists, a_blocks, b_blocks, c_prior)
-    a_last, mid_relay, c_now = lax.optimization_barrier((a[FIRST[2] :], mid_relay, c_now))
+    a_last, mid_relay, c_now = lax.optimization_barrier((a_inner[0, 0, FIRST[2] :], mid_relay, c_now))
     last_wrap = hop(a_last, DIRECT)
     mid_wrap = hop(mid_relay, FROM_2)
-    first, a_rest, c_now = lax.optimization_barrier((first, a[FIRST[1] :], c_now))
-    first_wrap = hop(first, FROM_3)
-    rest = hop(a_rest, INNER)
-    right, listing = pl.pallas_call(
+    first_wrap = hop(first_relay, FROM_3)
+    right, picked, listing = pl.pallas_call(
         halve_kernel,
         in_specs=[SMEM] * 5 + [HBM],
-        out_specs=[HBM, SMEM],
-        out_shape=[jax.ShapeDtypeStruct(wide, jnp.bfloat16), jax.ShapeDtypeStruct((3, 384), jnp.int32)],
+        out_specs=[HBM, VMEM, SMEM],
+        out_shape=[
+            jax.ShapeDtypeStruct(wide, jnp.bfloat16),
+            jax.ShapeDtypeStruct((BATCH, BS, 2 * BS), jnp.bfloat16),
+            jax.ShapeDtypeStruct((3, 384), jnp.int32),
+        ],
         scratch_shapes=[
             pltpu.VMEM(whole, jnp.float32),
             pltpu.VMEM(wide, jnp.bfloat16),
@@ -273,6 +290,7 @@
             pltpu.VMEM((BATCH, BS, BS), jnp.float32),
             pltpu.VMEM((BATCH, BS, 2 * BS), jnp.bfloat16),
             pltpu.VMEM((BS, BS), jnp.float32),
+            pltpu.VMEM((BS, BS), jnp.float32),
             pltpu.SemaphoreType.DMA,
             pltpu.SemaphoreType.DMA,
             pltpu.SemaphoreType.DMA,
@@ -280,11 +298,11 @@
         compiler_params=params,
         cost_estimate=pl.CostEstimate(flops=8 * BATCH * BS**3, bytes_accessed=MIB, transcendentals=0),
         name="trace_term",
-    )(listing, diag_slot, wraps, first, rest, last_wrap, mid_wrap, first_wrap, right, c_now)
+    )(listing, diag_slot, wraps, inner, last_wrap, mid_wrap, first_wrap, right, picked, c_now)
     terms = lax.all_to_all(term, AXES, 0, 0, tiled=True)
     c_now = pl.pallas_call(
         second_kernel,
-        in_specs=[SMEM] * 5 + [HBM] * 7,
+        in_specs=[SMEM] * 5 + [HBM] * 6,
         out_specs=HBM,
         out_shape=jax.ShapeDtypeStruct(whole, jnp.float32),
         scratch_shapes=[
@@ -297,7 +315,7 @@
         compiler_params=params,
         cost_estimate=cost,
         name="step1",
-    )(*lists, wraps, first, rest, last_wrap, mid_wrap, first_wrap, right, c_now)
+    )(*lists, wraps, inner, last_wrap, mid_wrap, first_wrap, right, c_now)
     trace_value = jnp.sum(terms[:, 0]) / (BS * jnp.sqrt(jnp.float32(devices)))
     return (c_now[None, None], trace_value)
 

time: 131 us -> 125 us (0.954)
  waiting for transfers between devices: 26 us -> 36.2 us
  Pallas kernels: 33.4 us -> 27.7 us
  local copies, waits for them, and re-layouts: 7.99 us -> 2.98 us
  starting transfers between devices: 58.8 us -> 54.2 us
    ppermute x6, waiting for transfers between devices: 23.2 us -> 31.4 us  [local(): hop = lambda array, pairs: lax.ppermute(array, AXES, pairs)]
    ppermute x6, starting transfers between devices: 28.3 us -> 20.5 us  [local(): hop = lambda array, pairs: lax.ppermute(array, AXES, pairs)]
    slice x4 -> x1, local copies, waits for them, and re-layouts: 6.32 us -> 1.91 us  [local(): a_first, a_mid = (a[:FIRST[1]], a[FIRST[1]:FIRST[2]])]
    pallas_call x1, Pallas kernels: 12.7 us -> 8.87 us  [local(): pl.pallas_call(first_kernel, in_specs=[SMEM] * 4 + [HBM] * 3, out_specs=H...]
    ppermute x1, starting transfers between devices: 0.96 us -> 3.32 us  [local(): b_next = lax.ppermute(b_sent, 'row', ROWS)]
    unnamed x4 -> x2, local copies, waits for them, and re-layouts: 1.67 us -> 0.01 us
  transfers between devices with their start and end apart: 8 -> 8, of which waited for: 5 -> 5; matrix products, arithmetic and copies ran while one was open for 4% -> 1% of each run, Pallas kernels for 22% -> 19%
where the time goes in v4:
time: 125 us
  starting transfers between devices  54.2 us (43%)
  waiting for transfers between devices  36.2 us (29%)
  Pallas kernels  27.7 us (22%)
  between operations  3.13 us (3%)
  local copies, waits for them, and re-layouts  2.98 us (2%)
    ppermute x6, waiting for transfers between devices, local(): hop = lambda array, pairs: lax.ppermute(array, AXES, pairs)  31.4 us
    all_to_all x1, starting transfers between devices, local(): terms = lax.all_to_all(term, AXES, 0, 0, tiled=True)  30.4 us
    ppermute x6, starting transfers between devices, local(): hop = lambda array, pairs: lax.ppermute(array, AXES, pairs)  20.5 us
    pallas_call x1, Pallas kernels, local(): pl.pallas_call(first_kernel, in_specs=[SMEM] * 4 + [HBM] * 3, out_specs=H...  8.87 us
    pallas_call x1, Pallas kernels, local(): pl.pallas_call(second_kernel, in_specs=[SMEM] * 5 + [HBM] * 6, out_specs=...  8.86 us
    pallas_call x1, Pallas kernels, local(): pl.pallas_call(halve_kernel, in_specs=[SMEM] * 5 + [HBM], out_specs=[HBM,...  5.99 us
    pallas_call x1, Pallas kernels, local(): pl.pallas_call(trace_kernel, in_specs=[SMEM] * 3 + [HBM] * 7, out_specs=V...  4.01 us
    all_to_all x1, waiting for transfers between devices, local(): terms = lax.all_to_all(term, AXES, 0, 0, tiled=True)  3.97 us
  transfers between devices with their start and end apart: 8, of which 5 were waited for; matrix products, arithmetic and copies ran while one was open for 1% of the time, Pallas kernels for 19%

profile of v4, /device:TPU:1, one launch (start us, length us, event | category | flops | bytes accessed | tf_op | source)
XLA Modules:
  0.0 124.8 jit_solution(17182288825552468120)
XLA Ops:
  0.6 0.0 copy-start
  0.6 1.9 %slice_bitcast_fusion.1 = (f32[16,128,128]{2,1,0:T(8,128)S(1)}, f32[16,128,128]{2,1,0:T(8,128)S(1)}) fusion(f32[1,1,48,128,128]{4,3,2,1,0:T(8,128)} %a_ref.1), kind=kLoop, calls=%fused_computation.1 | loop fusion | bytes 4194304 | tf_op jit(solution)/shard_map/slice | solution.py:236
  2.6 3.3 %collective-permute-start.3 = (f32[1,1,48,128,128]{4,3,2,1,0:T(8,128)}, f32[1,1,48,128,128]{4,3,2,1,0:T(8,128)}, u32[]{:S(2)}, u32[]{:S(2)}) collective-permute-start(f32[1,1,48,128,128]{4,3,2,1,0:T(8,128)} %b_ref.1), channel_id=1, source_target_pairs={{32,0},{64,32},{96,64},{128,96},{160,128},{192,160},{224,192},{0,2... | collective-permute-start | bytes 9437192 | tf_op jit(solution)/shard_map/ppermute | solution.py:241
  5.9 0.0 copy-done
  5.9 1.3 %collective-permute-start.4 = (f32[1,1,48,128,128]{4,3,2,1,0:T(8,128)S(1)}, f32[1,1,48,128,128]{4,3,2,1,0:T(8,128)}, u32[]{:S(2)}, u32[]{:S(2)}) collective-permute-start(f32[1,1,48,128,128]{4,3,2,1,0:T(8,128)S(1)} %copy-done), channel_id=1, source_target_pairs={{1,0},{2,1},{3,2},{5,4},{6,5},{7,6},{9,8},{10,9},{11,10},{13,12},{... | collective-permute-start | bytes 9437192 | tf_op jit(solution)/shard_map/ppermute | solution.py:228
  7.2 7.2 %collective-permute-start = (f32[16,128,128]{2,1,0:T(8,128)S(1)}, f32[16,128,128]{2,1,0:T(8,128)}, u32[]{:S(2)}, u32[]{:S(2)}) collective-permute-start(f32[16,128,128]{2,1,0:T(8,128)S(1)} %get-tuple-element.17), channel_id=1, source_target_pairs={{0,26},{4,6},{8,2},{12,14},{16,10},{20,22},{24,18},{28,30},{32,58}... | collective-permute-start | bytes 3145736 | tf_op jit(solution)/shard_map/ppermute | solution.py:228
  14.4 3.3 %collective-permute-start.5 = (f32[16,128,128]{2,1,0:T(8,128)S(1)}, f32[16,128,128]{2,1,0:T(8,128)}, u32[]{:S(2)}, u32[]{:S(2)}) collective-permute-start(f32[16,128,128]{2,1,0:T(8,128)S(1)} %get-tuple-element.25), channel_id=1, source_target_pairs={{0,27},{4,7},{8,3},{12,15},{16,11},{20,23},{24,19},{28,31},{32,59}... | collective-permute-start | bytes 3145736 | tf_op jit(solution)/shard_map/ppermute | solution.py:228
  17.7 1.1 slice_bitcast_fusion
  18.7 8.9 %step0.1.c_ref = f32[48,128,128]{2,1,0:T(8,128)} custom-call(s32[1,1,2,320]{3,2,1,0:T(2,128)} %idx_a.5, s32[1,1,2,320]{3,2,1,0:T(2,128)} %idx_b.5, s32[1,1,2,320]{3,2,1,0:T(2,128)} %idx_c.5, s32[1,1,2]{2,1,0:T(1,128)} %count.5, f32[1,1,48,128,128]{4,3,2,1,0:T(8,128)} %a_ref.1, f32[1,1,48,128,128]{4,3,2,1,0:T(8,128)} %b_ref.1, f32[1,1,48,128,128]{4,3,2,1,0:T(8,128)} %c_ref.1), custom_call_target="tpu_custom_call" | custom-call | flops 5368709120 | bytes 16777216 | tf_op jit(solution)/shard_map/step0/pallas_call | solution.py:242
  27.6 3.9 %collective-permute-done = f32[16,128,128]{2,1,0:T(8,128)} collective-permute-done((f32[16,128,128]{2,1,0:T(8,128)S(1)}, f32[16,128,128]{2,1,0:T(8,128)}, u32[]{:S(2)}, u32[]{:S(2)}) %collective-permute-start) | collective-permute-done | bytes 1048608 | tf_op jit(solution)/shard_map/ppermute | solution.py:228
  31.5 5.4 %collective-permute-start.1 = (f32[16,128,128]{2,1,0:T(8,128)}, f32[16,128,128]{2,1,0:T(8,128)}, u32[]{:S(2)}, u32[]{:S(2)}) collective-permute-start(f32[16,128,128]{2,1,0:T(8,128)} %slice_bitcast_fusion), channel_id=1, source_target_pairs={{0,31},{4,3},{8,7},{12,11},{16,15},{20,19},{24,23},{28,27},{32,63}... | collective-permute-start | bytes 3145736 | tf_op jit(solution)/shard_map/ppermute | solution.py:228
  36.9 1.6 %collective-permute-start.2 = (f32[16,128,128]{2,1,0:T(8,128)}, f32[16,128,128]{2,1,0:T(8,128)}, u32[]{:S(2)}, u32[]{:S(2)}) collective-permute-start(f32[16,128,128]{2,1,0:T(8,128)} %collective-permute-done), channel_id=1, source_target_pairs={{2,7},{6,3},{10,15},{14,11},{18,23},{22,19},{26,31},{30,27},{34,39... | collective-permute-start | bytes 3145736 | tf_op jit(solution)/shard_map/ppermute | solution.py:228
  38.5 0.0 collective-permute-done.5
  38.5 1.6 %collective-permute-start.6 = (f32[16,128,128]{2,1,0:T(8,128)}, f32[16,128,128]{2,1,0:T(8,128)}, u32[]{:S(2)}, u32[]{:S(2)}) collective-permute-start(f32[16,128,128]{2,1,0:T(8,128)} %collective-permute-done.5), channel_id=1, source_target_pairs={{3,7},{7,3},{11,15},{15,11},{19,23},{23,19},{27,31},{31,27},{35,39... | collective-permute-start | bytes 3145736 | tf_op jit(solution)/shard_map/ppermute | solution.py:228
  40.8 0.8 collective-permute-done.3.source
  41.7 6.0 %halves.1 = (bf16[48,128,256]{2,1,0:T(8,128)(2,1)}, bf16[16,128,256]{2,1,0:T(8,128)(2,1)}, s32[3,384]{1,0:T(4,128)}) custom-call(s32[1,1,2,320]{3,2,1,0:T(2,128)} %idx_a.5, s32[1,1,2,320]{3,2,1,0:T(2,128)} %idx_b.5, s32[1,1,2,320]{3,2,1,0:T(2,128)} %idx_c.5, s32[1,1,2]{2,1,0:T(1,128)} %count.5, s32[1,1]{1,0:T(1,128)S(6)} %copy.11.diag, ...), custom_call_target="tpu_custom_call" | custom-call | flops 1048576 | bytes 6291456 | tf_op jit(solution)/shard_map/halves/pallas_call | solution.py:263
  47.7 11.9 %collective-permute-done.1.last_wrap = f32[16,128,128]{2,1,0:T(8,128)} collective-permute-done((f32[16,128,128]{2,1,0:T(8,128)}, f32[16,128,128]{2,1,0:T(8,128)}, u32[]{:S(2)}, u32[]{:S(2)}) %collective-permute-start.1) | collective-permute-done | bytes 1048608 | tf_op jit(solution)/shard_map/ppermute | solution.py:228
  59.6 0.0 collective-permute-done.2.mid_wrap
  59.6 0.0 collective-permute-done.6.first_wrap
  59.6 15.5 %collective-permute-done.4.inner = f32[1,1,48,128,128]{4,3,2,1,0:T(8,128)} collective-permute-done((f32[1,1,48,128,128]{4,3,2,1,0:T(8,128)S(1)}, f32[1,1,48,128,128]{4,3,2,1,0:T(8,128)}, u32[]{:S(2)}, u32[]{:S(2)}) %collective-permute-start.4) | collective-permute-done | bytes 3145760 | tf_op jit(solution)/shard_map/ppermute | solution.py:228
  75.1 4.0 %trace_term.1 = f32[256,128]{1,0:T(8,128)} custom-call(s32[3,384]{1,0:T(4,128)} %get-tuple-element.28.listing, s32[1,1]{1,0:T(1,128)S(6)} %copy.11.diag, s32[1]{0:T(128)} %bitcast.wraps, f32[1,1,48,128,128]{4,3,2,1,0:T(8,128)} %collective-permute-done.4.inner, f32[16,128,128]{2,1,0:T(8,128)} %collective-permute-done.1.last_wrap, ...), custom_call_target="tpu_custom_call" | custom-call | flops 268435456 | bytes 1048576 | tf_op jit(solution)/shard_map/trace_term/pallas_call | solution.py:284
  79.2 30.4 %all-to-all-start = ((f32[256,1,128]{2,1,0:T(1,128)}), f32[256,1,128]{2,1,0:T(1,128)S(1)}, u32[]{:S(2)}, u32[]{:S(2)}) async-start(f32[256,1,128]{2,1,0:T(1,128)} %bitcast.12), calls=%async_computation | async-start | bytes 262144 | tf_op jit(solution)/shard_map/all_to_all | solution.py:302
  109.6 8.9 %step1.1 = f32[48,128,128]{2,1,0:T(8,128)} custom-call(s32[1,1,2,320]{3,2,1,0:T(2,128)} %idx_a.5, s32[1,1,2,320]{3,2,1,0:T(2,128)} %idx_b.5, s32[1,1,2,320]{3,2,1,0:T(2,128)} %idx_c.5, s32[1,1,2]{2,1,0:T(1,128)} %count.5, s32[1]{0:T(128)} %bitcast.wraps, f32[1,1,48,128,128]{4,3,2,1,0:T(8,128)} %collective-permute-done.4.inner, ...), custom_call_target="tpu_custom_call" | custom-call | flops 5368709120 | bytes 16777216 | tf_op jit(solution)/shard_map/step1/pallas_call | solution.py:303
  118.5 4.0 %all-to-all-done = f32[256,1,128]{2,1,0:T(1,128)S(1)} async-done(((f32[256,1,128]{2,1,0:T(1,128)}), f32[256,1,128]{2,1,0:T(1,128)S(1)}, u32[]{:S(2)}, u32[]{:S(2)}) %all-to-all-start) | async-done | bytes 131104 | tf_op jit(solution)/shard_map/all_to_all | solution.py:302
  122.4 0.6 slice_reduce_fusion
Async XLA Ops:
  0.6 5.2 %copy-start = (f32[1,1,48,128,128]{4,3,2,1,0:T(8,128)S(1)}, f32[1,1,48,128,128]{4,3,2,1,0:T(8,128)}, u32[]{:S(2)}) copy-start(f32[1,1,48,128,128]{4,3,2,1,0:T(8,128)} %a_ref.1) | copy-start | bytes 9437188
  2.6 39.1 %collective-permute-start.3 = (f32[1,1,48,128,128]{4,3,2,1,0:T(8,128)}, f32[1,1,48,128,128]{4,3,2,1,0:T(8,128)}, u32[]{:S(2)}, u32[]{:S(2)}) collective-permute-start(f32[1,1,48,128,128]{4,3,2,1,0:T(8,128)} %b_ref.1), channel_id=1, source_target_pairs={{32,0},{64,32},{96,64},{128,96},{160,128},{192,160},{224,192},{0,2... | collective-permute-start | bytes 9437192 | tf_op jit(solution)/shard_map/ppermute | solution.py:241
  5.9 69.3 %collective-permute-start.4 = (f32[1,1,48,128,128]{4,3,2,1,0:T(8,128)S(1)}, f32[1,1,48,128,128]{4,3,2,1,0:T(8,128)}, u32[]{:S(2)}, u32[]{:S(2)}) collective-permute-start(f32[1,1,48,128,128]{4,3,2,1,0:T(8,128)S(1)} %copy-done), channel_id=1, source_target_pairs={{1,0},{2,1},{3,2},{5,4},{6,5},{7,6},{9,8},{10,9},{11,10},{13,12},{... | collective-permute-start | bytes 9437192 | tf_op jit(solution)/shard_map/ppermute | solution.py:228
  7.2 24.3 %collective-permute-start = (f32[16,128,128]{2,1,0:T(8,128)S(1)}, f32[16,128,128]{2,1,0:T(8,128)}, u32[]{:S(2)}, u32[]{:S(2)}) collective-permute-start(f32[16,128,128]{2,1,0:T(8,128)S(1)} %get-tuple-element.17), channel_id=1, source_target_pairs={{0,26},{4,6},{8,2},{12,14},{16,10},{20,22},{24,18},{28,30},{32,58}... | collective-permute-start | bytes 3145736 | tf_op jit(solution)/shard_map/ppermute | solution.py:228
  14.4 24.2 %collective-permute-start.5 = (f32[16,128,128]{2,1,0:T(8,128)S(1)}, f32[16,128,128]{2,1,0:T(8,128)}, u32[]{:S(2)}, u32[]{:S(2)}) collective-permute-start(f32[16,128,128]{2,1,0:T(8,128)S(1)} %get-tuple-element.25), channel_id=1, source_target_pairs={{0,27},{4,7},{8,3},{12,15},{16,11},{20,23},{24,19},{28,31},{32,59}... | collective-permute-start | bytes 3145736 | tf_op jit(solution)/shard_map/ppermute | solution.py:228
  31.5 28.1 %collective-permute-start.1 = (f32[16,128,128]{2,1,0:T(8,128)}, f32[16,128,128]{2,1,0:T(8,128)}, u32[]{:S(2)}, u32[]{:S(2)}) collective-permute-start(f32[16,128,128]{2,1,0:T(8,128)} %slice_bitcast_fusion), channel_id=1, source_target_pairs={{0,31},{4,3},{8,7},{12,11},{16,15},{20,19},{24,23},{28,27},{32,63}... | collective-permute-start | bytes 3145736 | tf_op jit(solution)/shard_map/ppermute | solution.py:228
  36.9 22.7 %collective-permute-start.2 = (f32[16,128,128]{2,1,0:T(8,128)}, f32[16,128,128]{2,1,0:T(8,128)}, u32[]{:S(2)}, u32[]{:S(2)}) collective-permute-start(f32[16,128,128]{2,1,0:T(8,128)} %collective-permute-done), channel_id=1, source_target_pairs={{2,7},{6,3},{10,15},{14,11},{18,23},{22,19},{26,31},{30,27},{34,39... | collective-permute-start | bytes 3145736 | tf_op jit(solution)/shard_map/ppermute | solution.py:228
  38.5 21.1 %collective-permute-start.6 = (f32[16,128,128]{2,1,0:T(8,128)}, f32[16,128,128]{2,1,0:T(8,128)}, u32[]{:S(2)}, u32[]{:S(2)}) collective-permute-start(f32[16,128,128]{2,1,0:T(8,128)} %collective-permute-done.5), channel_id=1, source_target_pairs={{3,7},{7,3},{11,15},{15,11},{19,23},{23,19},{27,31},{31,27},{35,39... | collective-permute-start | bytes 3145736 | tf_op jit(solution)/shard_map/ppermute | solution.py:228
  79.2 43.3 %all-to-all-start = ((f32[256,1,128]{2,1,0:T(1,128)}), f32[256,1,128]{2,1,0:T(1,128)S(1)}, u32[]{:S(2)}, u32[]{:S(2)}) async-start(f32[256,1,128]{2,1,0:T(1,128)} %bitcast.12), calls=%async_computation | async-start | bytes 262144 | tf_op jit(solution)/shard_map/all_to_all | solution.py:302

commit v5 on v4

--- a/solution.py
+++ b/solution.py
@@ -203,11 +203,13 @@
 
         pltpu.make_async_copy(picked, b_in, b_sem).wait()
         pltpu.make_async_copy(inner.at[0, 0, pl.ds(0, BATCH)], a_in, a_sem).wait()
+        sums = total[...]
         for i in range(BATCH):
             halves = jnp.concatenate(split(a_in[i]), axis=1)
             weights = b_in[i]
             both = jnp.dot(halves, jnp.concatenate([weights, weights], axis=0), preferred_element_type=jnp.float32)
-            total[...] += jnp.where(g * BATCH + i < found, both[:, :BS] + both[:, BS:], 0.0)
+            sums = sums + jnp.where(g * BATCH + i < found, both[:, :BS] + both[:, BS:], 0.0)
+        total[...] = sums
         return carry
 
     lax.fori_loop(0, lax.div(found + BATCH - 1, BATCH), batch, 0)
@@ -256,7 +258,7 @@
         cost_estimate=cost,
         name="step0",
     )(*lists, a_blocks, b_blocks, c_prior)
-    a_last, mid_relay, c_now = lax.optimization_barrier((a_inner[0, 0, FIRST[2] :], mid_relay, c_now))
+    a_last, mid_relay = lax.optimization_barrier((a_inner[0, 0, FIRST[2] :], mid_relay))
     last_wrap = hop(a_last, DIRECT)
     mid_wrap = hop(mid_relay, FROM_2)
     first_wrap = hop(first_relay, FROM_3)

time: 125 us -> 126 us (level)
  Pallas kernels: 27.7 us -> 30 us
    ppermute x6, starting transfers between devices: 20.5 us -> 17.4 us  [local(): hop = lambda array, pairs: lax.ppermute(array, AXES, pairs)]
    pallas_call x1, Pallas kernels: 8.87 us -> 11.5 us  [local(): pl.pallas_call(first_kernel, in_specs=[SMEM] * 4 + [HBM] * 3, out_specs=H...]
    all_to_all x1, starting transfers between devices: 30.4 us -> 32.5 us  [local(): terms = lax.all_to_all(term, AXES, 0, 0, tiled=True)]
    pallas_call x1, Pallas kernels: 4.01 us -> 2.41 us  [local(): pl.pallas_call(trace_kernel, in_specs=[SMEM] * 3 + [HBM] * 7, out_specs=V...]
    ppermute x6, waiting for transfers between devices: 31.4 us -> 32.7 us  [local(): hop = lambda array, pairs: lax.ppermute(array, AXES, pairs)]
    all_to_all x1, waiting for transfers between devices: 3.97 us -> 2.7 us  [local(): terms = lax.all_to_all(term, AXES, 0, 0, tiled=True)]
    pallas_call x1, Pallas kernels: 8.86 us -> 10.1 us  [local(): pl.pallas_call(second_kernel, in_specs=[SMEM] * 5 + [HBM] * 6, out_specs=...]
  transfers between devices with their start and end apart: 8 -> 8, of which waited for: 5 -> 4; matrix products, arithmetic and copies ran while one was open for 1% -> 1% of each run, Pallas kernels for 19% -> 22%
where the time goes in v5:
time: 126 us; the launch traced here: 125 us
  starting transfers between devices  53.2 us (42%)
  waiting for transfers between devices  35.4 us (28%)
  Pallas kernels  30 us (24%)
  between operations  3.14 us (2%)
  local copies, waits for them, and re-layouts  2.9 us (2%)
    ppermute x6, waiting for transfers between devices, local(): hop = lambda array, pairs: lax.ppermute(array, AXES, pairs)  32.7 us
    all_to_all x1, starting transfers between devices, local(): terms = lax.all_to_all(term, AXES, 0, 0, tiled=True)  32.5 us
    ppermute x6, starting transfers between devices, local(): hop = lambda array, pairs: lax.ppermute(array, AXES, pairs)  17.4 us
    pallas_call x1, Pallas kernels, local(): pl.pallas_call(first_kernel, in_specs=[SMEM] * 4 + [HBM] * 3, out_specs=H...  11.5 us
    pallas_call x1, Pallas kernels, local(): pl.pallas_call(second_kernel, in_specs=[SMEM] * 5 + [HBM] * 6, out_specs=...  10.1 us
    pallas_call x1, Pallas kernels, local(): pl.pallas_call(halve_kernel, in_specs=[SMEM] * 5 + [HBM], out_specs=[HBM,...  5.99 us
    ppermute x1, starting transfers between devices, local(): b_next = lax.ppermute(b_sent, 'row', ROWS)  3.32 us
    all_to_all x1, waiting for transfers between devices, local(): terms = lax.all_to_all(term, AXES, 0, 0, tiled=True)  2.7 us
  transfers between devices with their start and end apart: 8, of which 4 were waited for; matrix products, arithmetic and copies ran while one was open for 1% of the time, Pallas kernels for 22%

profile of v5, /device:TPU:1, one launch (start us, length us, event | category | flops | bytes accessed | tf_op | source)
XLA Modules:
  0.0 125.2 jit_solution(2857154125077162352)
XLA Ops:
  0.6 0.0 copy-start
  0.6 1.8 %slice_bitcast_fusion.1 = (f32[16,128,128]{2,1,0:T(8,128)S(1)}, f32[16,128,128]{2,1,0:T(8,128)S(1)}) fusion(f32[1,1,48,128,128]{4,3,2,1,0:T(8,128)} %a_ref.1), kind=kLoop, calls=%fused_computation.1 | loop fusion | bytes 4194304 | tf_op jit(solution)/shard_map/slice | solution.py:238
  2.5 3.3 %collective-permute-start.3 = (f32[1,1,48,128,128]{4,3,2,1,0:T(8,128)}, f32[1,1,48,128,128]{4,3,2,1,0:T(8,128)}, u32[]{:S(2)}, u32[]{:S(2)}) collective-permute-start(f32[1,1,48,128,128]{4,3,2,1,0:T(8,128)} %b_ref.1), channel_id=1, source_target_pairs={{32,0},{64,32},{96,64},{128,96},{160,128},{192,160},{224,192},{0,2... | collective-permute-start | bytes 9437192 | tf_op jit(solution)/shard_map/ppermute | solution.py:243
  5.8 0.0 copy-done
  5.8 1.3 %collective-permute-start.4 = (f32[1,1,48,128,128]{4,3,2,1,0:T(8,128)S(1)}, f32[1,1,48,128,128]{4,3,2,1,0:T(8,128)}, u32[]{:S(2)}, u32[]{:S(2)}) collective-permute-start(f32[1,1,48,128,128]{4,3,2,1,0:T(8,128)S(1)} %copy-done), channel_id=1, source_target_pairs={{1,0},{2,1},{3,2},{5,4},{6,5},{7,6},{9,8},{10,9},{11,10},{13,12},{... | collective-permute-start | bytes 9437192 | tf_op jit(solution)/shard_map/ppermute | solution.py:230
  7.1 7.2 %collective-permute-start = (f32[16,128,128]{2,1,0:T(8,128)S(1)}, f32[16,128,128]{2,1,0:T(8,128)}, u32[]{:S(2)}, u32[]{:S(2)}) collective-permute-start(f32[16,128,128]{2,1,0:T(8,128)S(1)} %get-tuple-element.16), channel_id=1, source_target_pairs={{0,26},{4,6},{8,2},{12,14},{16,10},{20,22},{24,18},{28,30},{32,58}... | collective-permute-start | bytes 3145736 | tf_op jit(solution)/shard_map/ppermute | solution.py:230
  14.3 3.3 %collective-permute-start.5 = (f32[16,128,128]{2,1,0:T(8,128)S(1)}, f32[16,128,128]{2,1,0:T(8,128)}, u32[]{:S(2)}, u32[]{:S(2)}) collective-permute-start(f32[16,128,128]{2,1,0:T(8,128)S(1)} %get-tuple-element.24), channel_id=1, source_target_pairs={{0,27},{4,7},{8,3},{12,15},{16,11},{20,23},{24,19},{28,31},{32,59}... | collective-permute-start | bytes 3145736 | tf_op jit(solution)/shard_map/ppermute | solution.py:230
  17.6 1.1 slice_bitcast_fusion
  18.7 12.8 %collective-permute-done = f32[16,128,128]{2,1,0:T(8,128)} collective-permute-done((f32[16,128,128]{2,1,0:T(8,128)S(1)}, f32[16,128,128]{2,1,0:T(8,128)}, u32[]{:S(2)}, u32[]{:S(2)}) %collective-permute-start) | collective-permute-done | bytes 1048608 | tf_op jit(solution)/shard_map/ppermute | solution.py:230
  31.4 2.3 %collective-permute-start.1 = (f32[16,128,128]{2,1,0:T(8,128)}, f32[16,128,128]{2,1,0:T(8,128)}, u32[]{:S(2)}, u32[]{:S(2)}) collective-permute-start(f32[16,128,128]{2,1,0:T(8,128)} %slice_bitcast_fusion), channel_id=1, source_target_pairs={{0,31},{4,3},{8,7},{12,11},{16,15},{20,19},{24,23},{28,27},{32,63}... | collective-permute-start | bytes 3145736 | tf_op jit(solution)/shard_map/ppermute | solution.py:230
  33.7 1.6 %collective-permute-start.2 = (f32[16,128,128]{2,1,0:T(8,128)}, f32[16,128,128]{2,1,0:T(8,128)}, u32[]{:S(2)}, u32[]{:S(2)}) collective-permute-start(f32[16,128,128]{2,1,0:T(8,128)} %collective-permute-done), channel_id=1, source_target_pairs={{2,7},{6,3},{10,15},{14,11},{18,23},{22,19},{26,31},{30,27},{34,39... | collective-permute-start | bytes 3145736 | tf_op jit(solution)/shard_map/ppermute | solution.py:230
  35.4 0.0 collective-permute-done.5
  35.4 1.6 %collective-permute-start.6 = (f32[16,128,128]{2,1,0:T(8,128)}, f32[16,128,128]{2,1,0:T(8,128)}, u32[]{:S(2)}, u32[]{:S(2)}) collective-permute-start(f32[16,128,128]{2,1,0:T(8,128)} %collective-permute-done.5), channel_id=1, source_target_pairs={{3,7},{7,3},{11,15},{15,11},{19,23},{23,19},{27,31},{31,27},{35,39... | collective-permute-start | bytes 3145736 | tf_op jit(solution)/shard_map/ppermute | solution.py:230
  37.7 11.5 %step0.1.c_ref = f32[48,128,128]{2,1,0:T(8,128)} custom-call(s32[1,1,2,320]{3,2,1,0:T(2,128)} %idx_a.5, s32[1,1,2,320]{3,2,1,0:T(2,128)} %idx_b.5, s32[1,1,2,320]{3,2,1,0:T(2,128)} %idx_c.5, s32[1,1,2]{2,1,0:T(1,128)} %count.5, f32[1,1,48,128,128]{4,3,2,1,0:T(8,128)} %a_ref.1, f32[1,1,48,128,128]{4,3,2,1,0:T(8,128)} %b_ref.1, f32[1,1,48,128,128]{4,3,2,1,0:T(8,128)} %c_ref.1), custom_call_target="tpu_custom_call" | custom-call | flops 5368709120 | bytes 16777216 | tf_op jit(solution)/shard_map/step0/pallas_call | solution.py:244
  49.1 0.0 collective-permute-done.3.source
  49.2 6.0 %halves.1 = (bf16[48,128,256]{2,1,0:T(8,128)(2,1)}, bf16[16,128,256]{2,1,0:T(8,128)(2,1)}, s32[3,384]{1,0:T(4,128)}) custom-call(s32[1,1,2,320]{3,2,1,0:T(2,128)} %idx_a.5, s32[1,1,2,320]{3,2,1,0:T(2,128)} %idx_b.5, s32[1,1,2,320]{3,2,1,0:T(2,128)} %idx_c.5, s32[1,1,2]{2,1,0:T(1,128)} %count.5, s32[1,1]{1,0:T(1,128)S(6)} %copy.11.diag, ...), custom_call_target="tpu_custom_call" | custom-call | flops 1048576 | bytes 6291456 | tf_op jit(solution)/shard_map/halves/pallas_call | solution.py:265
  55.2 1.1 collective-permute-done.1.last_wrap
  56.3 0.0 collective-permute-done.2.mid_wrap
  56.3 0.0 collective-permute-done.6.first_wrap
  56.3 18.8 %collective-permute-done.4.inner = f32[1,1,48,128,128]{4,3,2,1,0:T(8,128)} collective-permute-done((f32[1,1,48,128,128]{4,3,2,1,0:T(8,128)S(1)}, f32[1,1,48,128,128]{4,3,2,1,0:T(8,128)}, u32[]{:S(2)}, u32[]{:S(2)}) %collective-permute-start.4) | collective-permute-done | bytes 3145760 | tf_op jit(solution)/shard_map/ppermute | solution.py:230
  75.1 2.4 %trace_term.1 = f32[256,128]{1,0:T(8,128)} custom-call(s32[3,384]{1,0:T(4,128)} %get-tuple-element.26.listing, s32[1,1]{1,0:T(1,128)S(6)} %copy.11.diag, s32[1]{0:T(128)} %bitcast.wraps, f32[1,1,48,128,128]{4,3,2,1,0:T(8,128)} %collective-permute-done.4.inner, f32[16,128,128]{2,1,0:T(8,128)} %collective-permute-done.1.last_wrap, ...), custom_call_target="tpu_custom_call" | custom-call | flops 268435456 | bytes 1048576 | tf_op jit(solution)/shard_map/trace_term/pallas_call | solution.py:286
  77.5 32.5 %all-to-all-start = ((f32[256,1,128]{2,1,0:T(1,128)}), f32[256,1,128]{2,1,0:T(1,128)S(1)}, u32[]{:S(2)}, u32[]{:S(2)}) async-start(f32[256,1,128]{2,1,0:T(1,128)} %bitcast.12), calls=%async_computation | async-start | bytes 262144 | tf_op jit(solution)/shard_map/all_to_all | solution.py:304
  110.0 10.1 %step1.1 = f32[48,128,128]{2,1,0:T(8,128)} custom-call(s32[1,1,2,320]{3,2,1,0:T(2,128)} %idx_a.5, s32[1,1,2,320]{3,2,1,0:T(2,128)} %idx_b.5, s32[1,1,2,320]{3,2,1,0:T(2,128)} %idx_c.5, s32[1,1,2]{2,1,0:T(1,128)} %count.5, s32[1]{0:T(128)} %bitcast.wraps, f32[1,1,48,128,128]{4,3,2,1,0:T(8,128)} %collective-permute-done.4.inner, ...), custom_call_target="tpu_custom_call" | custom-call | flops 5368709120 | bytes 16777216 | tf_op jit(solution)/shard_map/step1/pallas_call | solution.py:305
  120.1 2.7 %all-to-all-done = f32[256,1,128]{2,1,0:T(1,128)S(1)} async-done(((f32[256,1,128]{2,1,0:T(1,128)}), f32[256,1,128]{2,1,0:T(1,128)S(1)}, u32[]{:S(2)}, u32[]{:S(2)}) %all-to-all-start) | async-done | bytes 131104 | tf_op jit(solution)/shard_map/all_to_all | solution.py:304
  122.8 0.6 slice_reduce_fusion
Async XLA Ops:
  0.6 5.2 %copy-start = (f32[1,1,48,128,128]{4,3,2,1,0:T(8,128)S(1)}, f32[1,1,48,128,128]{4,3,2,1,0:T(8,128)}, u32[]{:S(2)}) copy-start(f32[1,1,48,128,128]{4,3,2,1,0:T(8,128)} %a_ref.1) | copy-start | bytes 9437188
  2.5 46.7 %collective-permute-start.3 = (f32[1,1,48,128,128]{4,3,2,1,0:T(8,128)}, f32[1,1,48,128,128]{4,3,2,1,0:T(8,128)}, u32[]{:S(2)}, u32[]{:S(2)}) collective-permute-start(f32[1,1,48,128,128]{4,3,2,1,0:T(8,128)} %b_ref.1), channel_id=1, source_target_pairs={{32,0},{64,32},{96,64},{128,96},{160,128},{192,160},{224,192},{0,2... | collective-permute-start | bytes 9437192 | tf_op jit(solution)/shard_map/ppermute | solution.py:243
  5.8 69.3 %collective-permute-start.4 = (f32[1,1,48,128,128]{4,3,2,1,0:T(8,128)S(1)}, f32[1,1,48,128,128]{4,3,2,1,0:T(8,128)}, u32[]{:S(2)}, u32[]{:S(2)}) collective-permute-start(f32[1,1,48,128,128]{4,3,2,1,0:T(8,128)S(1)} %copy-done), channel_id=1, source_target_pairs={{1,0},{2,1},{3,2},{5,4},{6,5},{7,6},{9,8},{10,9},{11,10},{13,12},{... | collective-permute-start | bytes 9437192 | tf_op jit(solution)/shard_map/ppermute | solution.py:230
  7.1 24.3 %collective-permute-start = (f32[16,128,128]{2,1,0:T(8,128)S(1)}, f32[16,128,128]{2,1,0:T(8,128)}, u32[]{:S(2)}, u32[]{:S(2)}) collective-permute-start(f32[16,128,128]{2,1,0:T(8,128)S(1)} %get-tuple-element.16), channel_id=1, source_target_pairs={{0,26},{4,6},{8,2},{12,14},{16,10},{20,22},{24,18},{28,30},{32,58}... | collective-permute-start | bytes 3145736 | tf_op jit(solution)/shard_map/ppermute | solution.py:230
  14.3 21.1 %collective-permute-start.5 = (f32[16,128,128]{2,1,0:T(8,128)S(1)}, f32[16,128,128]{2,1,0:T(8,128)}, u32[]{:S(2)}, u32[]{:S(2)}) collective-permute-start(f32[16,128,128]{2,1,0:T(8,128)S(1)} %get-tuple-element.24), channel_id=1, source_target_pairs={{0,27},{4,7},{8,3},{12,15},{16,11},{20,23},{24,19},{28,31},{32,59}... | collective-permute-start | bytes 3145736 | tf_op jit(solution)/shard_map/ppermute | solution.py:230
  31.4 24.8 %collective-permute-start.1 = (f32[16,128,128]{2,1,0:T(8,128)}, f32[16,128,128]{2,1,0:T(8,128)}, u32[]{:S(2)}, u32[]{:S(2)}) collective-permute-start(f32[16,128,128]{2,1,0:T(8,128)} %slice_bitcast_fusion), channel_id=1, source_target_pairs={{0,31},{4,3},{8,7},{12,11},{16,15},{20,19},{24,23},{28,27},{32,63}... | collective-permute-start | bytes 3145736 | tf_op jit(solution)/shard_map/ppermute | solution.py:230
  33.7 22.5 %collective-permute-start.2 = (f32[16,128,128]{2,1,0:T(8,128)}, f32[16,128,128]{2,1,0:T(8,128)}, u32[]{:S(2)}, u32[]{:S(2)}) collective-permute-start(f32[16,128,128]{2,1,0:T(8,128)} %collective-permute-done), channel_id=1, source_target_pairs={{2,7},{6,3},{10,15},{14,11},{18,23},{22,19},{26,31},{30,27},{34,39... | collective-permute-start | bytes 3145736 | tf_op jit(solution)/shard_map/ppermute | solution.py:230
  35.4 20.9 %collective-permute-start.6 = (f32[16,128,128]{2,1,0:T(8,128)}, f32[16,128,128]{2,1,0:T(8,128)}, u32[]{:S(2)}, u32[]{:S(2)}) collective-permute-start(f32[16,128,128]{2,1,0:T(8,128)} %collective-permute-done.5), channel_id=1, source_target_pairs={{3,7},{7,3},{11,15},{15,11},{19,23},{23,19},{27,31},{31,27},{35,39... | collective-permute-start | bytes 3145736 | tf_op jit(solution)/shard_map/ppermute | solution.py:230
  77.5 45.4 %all-to-all-start = ((f32[256,1,128]{2,1,0:T(1,128)}), f32[256,1,128]{2,1,0:T(1,128)S(1)}, u32[]{:S(2)}, u32[]{:S(2)}) async-start(f32[256,1,128]{2,1,0:T(1,128)} %bitcast.12), calls=%async_computation | async-start | bytes 262144 | tf_op jit(solution)/shard_map/all_to_all | solution.py:304
